TPU v7x, 32 devices: a whole 2x2x4 slice. The times are simulated.
32 devices in a mesh: dp: 4 (over z), expert: 8 (over y, x, core).
Axes of the slice: x: 2, y: 2, z: 4, core: 2. Of those that a mesh axis runs over, the one named last changes fastest.
Arguments:
- tokens: bfloat16 [30976, 768], P(('dp', 'expert')), may hold values from -6 to 6
- first_gain: float32 [768], replicated, may hold values from 0.5 to 1.5
- first_shift: float32 [768], replicated, may hold values from -0.6 to 0.6
- query_weight: bfloat16 [768, 768], replicated, may hold values from -0.21875 to 0.21875
- query_bias: float32 [768], replicated, may hold values from -0.6 to 0.6
- key_weight: bfloat16 [768, 768], replicated, may hold values from -0.21875 to 0.21875
- value_weight: bfloat16 [768, 768], replicated, may hold values from -0.21875 to 0.21875
- value_bias: float32 [768], replicated, may hold values from -0.6 to 0.6
- out_weight: bfloat16 [768, 768], replicated, may hold values from -3.5 to 3.5
- out_bias: float32 [768], replicated, may hold values from -0.6 to 0.6
- second_gain: float32 [768], replicated, may hold values from 0.5 to 1.5
- second_shift: float32 [768], replicated, may hold values from -0.6 to 0.6
- router: bfloat16 [768, 8], replicated, may hold values from -0.15625 to 0.15625
- expert_up: bfloat16 [8, 768, 3072], P('expert'), may hold values from -0.21875 to 0.21875
- expert_up_bias: float32 [8, 3072], P('expert'), may hold values from -0.6 to 0.6
- expert_down: bfloat16 [8, 3072, 768], P('expert'), may hold values from -1.75 to 1.75
- expert_down_bias: float32 [8, 768], P('expert'), may hold values from -6 to 6
- choices: int32 [30976, 2], P(('dp', 'expert')), may hold values from 0 to 7, all different within a row; in each aligned block of 968 rows (0 to 967, 968 to 1935, ...) at most 384 rows name the same one
- priority: int32 [32, 968], P(('dp', 'expert')), may hold values from 0 to 967, each once within a row
- cotangent: bfloat16 [30976, 768], P(('dp', 'expert')), may hold values from -6 to 6
Outputs:
- block_output: bfloat16 [30976, 768], P(('dp', 'expert'))
- input_grad: bfloat16 [30976, 768], P(('dp', 'expert'))
- first_gain_grad: float32 [768], replicated
- first_shift_grad: float32 [768], replicated
- query_weight_grad: float32 [768, 768], replicated
- query_bias_grad: float32 [768], replicated
- key_weight_grad: float32 [768, 768], replicated
- value_weight_grad: float32 [768, 768], replicated
- value_bias_grad: float32 [768], replicated
- out_weight_grad: float32 [768, 768], replicated
- out_bias_grad: float32 [768], replicated
- second_gain_grad: float32 [768], replicated
- second_shift_grad: float32 [768], replicated
- router_grad: float32 [768, 8], replicated
- expert_up_grad: float32 [8, 768, 3072], P('expert', 'dp')
- expert_up_bias_grad: float32 [8, 3072], P('expert', 'dp')
- expert_down_grad: float32 [8, 3072, 768], P('expert', 'dp')
- expert_down_bias_grad: float32 [8, 768], P('expert', 'dp')
Inputs may be any that keep to these rules, and one draw needn't show every extreme that they name: `choices`: the two experts of a patch differ; among the pairs of one device's patches no expert is named more than 384 times. `priority`: each row holds every number from 0 to 967 once.
All inputs are finite; a program needn't handle non-finite values.
Results may differ from a plain program's by a relative error of at most 0.015.
Values may be sent and summed in bfloat16 or wider, within the bound.
No kernel may reach another device: no remote copies, remote signals or barrier semaphores. Data moves between devices by JAX's collectives and lax.ppermute only.
A program may use at most 320 MiB of HBM per device.

v0:
```python
import jax
import jax.numpy as jnp
from jax import lax
from jax.sharding import PartitionSpec as P

HEADS = 12
BIG = 576
SMALL = 196


half_type = jnp.bfloat16
full_type = jnp.float32
norm_eps = 1e-06
masked_score = -1000000000.0


def dot_low(left, right):
    return jnp.dot(left, right, preferred_element_type=full_type)


def dot_full(left, right):
    return jnp.dot(left, right, precision=lax.Precision.HIGHEST, preferred_element_type=full_type)


def gelu_exact(values):
    return jax.nn.gelu(values, approximate=False)


def layer_norm(values, norm_gain, norm_shift):
    row_mean = jnp.mean(values, axis=-1, keepdims=True)
    centered = values - row_mean
    inverse = lax.rsqrt(jnp.mean(centered * centered, axis=-1, keepdims=True) + norm_eps)
    normed = centered * inverse
    return (normed * norm_gain + norm_shift, normed, inverse)


def norm_backward(upstream, normed, inverse, norm_gain):
    scaled = upstream * norm_gain
    first_mean = jnp.mean(scaled, axis=-1, keepdims=True)
    second_mean = jnp.mean(scaled * normed, axis=-1, keepdims=True)
    grad_input = inverse * (scaled - first_mean - normed * second_mean)
    return (grad_input, jnp.sum(upstream * normed, axis=0), jnp.sum(upstream, axis=0))


def image_ids(tok_count):
    position = jnp.arange(tok_count, dtype=jnp.int32)
    return jnp.where(position < BIG, 0, 1 + (position - BIG) // SMALL)


def slot_table(choice_rows, priority_row, expert_count, capacity):
    tok_count = priority_row.shape[0]
    order_key = jnp.concatenate([priority_row, priority_row + tok_count])
    expert_flat = jnp.concatenate([choice_rows[:, 0], choice_rows[:, 1]])
    by_key = jnp.zeros((2 * tok_count,), jnp.int32).at[order_key].set(expert_flat)
    onehot = (by_key[:, None] == jnp.arange(expert_count, dtype=jnp.int32)[None, :]).astype(
        jnp.int32
    )
    before = jnp.cumsum(onehot, axis=0) - onehot
    place_by_key = jnp.sum(before * onehot, axis=1)
    place = place_by_key[order_key]
    kept_mask = place < capacity
    slot_index = jnp.where(kept_mask, expert_flat * capacity + place, expert_count * capacity)
    return (slot_index.reshape(2, tok_count).T, kept_mask.reshape(2, tok_count).T)


def attn_scores(query3, key3, allowed, score_scale):
    raw = jnp.einsum("qhd,khd->hqk", query3, key3, preferred_element_type=full_type) * score_scale
    return jnp.where(allowed[None], raw, masked_score)


def shards(
    tokens,
    first_gain,
    first_shift,
    query_weight,
    query_bias,
    key_weight,
    value_weight,
    value_bias,
    out_weight,
    out_bias,
    second_gain,
    second_shift,
    router,
    expert_up,
    expert_up_bias,
    expert_down,
    expert_down_bias,
    choices,
    priority,
    cotangent,
):
    tok_count, feat_width = tokens.shape
    head_count = HEADS
    head_size = feat_width // head_count
    expert_count = lax.axis_size("expert")
    capacity = (21 * tok_count + 80 * expert_count - 1) // (80 * expert_count) * 8
    slot_total = expert_count * capacity
    score_scale = head_size ** (-0.5)
    image = image_ids(tok_count)
    allowed = image[:, None] == image[None, :]
    resid = tokens.astype(full_type)
    first_out, first_normed, first_inverse = layer_norm(resid, first_gain, first_shift)
    first_low = first_out.astype(half_type)
    query_low = (dot_low(first_low, query_weight) + query_bias).astype(half_type)
    key_low = dot_low(first_low, key_weight).astype(half_type)
    value_low = (dot_low(first_low, value_weight) + value_bias).astype(half_type)
    query3 = query_low.reshape(tok_count, head_count, head_size)
    key3 = key_low.reshape(tok_count, head_count, head_size)
    value3 = value_low.reshape(tok_count, head_count, head_size)
    scores = attn_scores(query3, key3, allowed, score_scale)
    row_max = jnp.max(scores, axis=-1, keepdims=True)
    log_total = row_max + jnp.log(jnp.sum(jnp.exp(scores - row_max), axis=-1, keepdims=True))
    weights_low = jnp.exp(scores - log_total).astype(half_type)
    attended = (
        jnp.einsum("hqk,khd->qhd", weights_low, value3, preferred_element_type=full_type)
        .reshape(tok_count, feat_width)
        .astype(half_type)
    )
    middle = resid + dot_low(attended, out_weight) + out_bias
    second_out, second_normed, second_inverse = layer_norm(middle, second_gain, second_shift)
    second_low = second_out.astype(half_type)
    router_probs = jax.nn.softmax(dot_low(second_low, router), axis=-1)
    slot_index, kept_mask = slot_table(choices, priority[0], expert_count, capacity)
    kept_float = kept_mask.astype(full_type)
    gate_values = jnp.take_along_axis(router_probs, choices, axis=1) * kept_float
    pair_owner = (
        jnp.full((slot_total,), 2 * tok_count, jnp.int32)
        .at[slot_index.reshape(-1)]
        .set(jnp.arange(2 * tok_count, dtype=jnp.int32), mode="drop")
    )
    token_owner = pair_owner // 2
    padded_two = jnp.concatenate([second_low, jnp.zeros((1, feat_width), half_type)])
    sent = padded_two[token_owner].reshape(expert_count, capacity, feat_width)
    up_local = expert_up[0]
    up_bias_local = expert_up_bias[0]
    down_local = expert_down[0]
    down_bias_local = expert_down_bias[0]
    received = lax.all_to_all(sent, "expert", split_axis=0, concat_axis=0, tiled=True)
    block_rows = received.reshape(-1, feat_width)
    pre_act = dot_low(block_rows, up_local) + up_bias_local
    act_low = gelu_exact(pre_act).astype(half_type)
    result = (dot_low(act_low, down_local) + down_bias_local).astype(half_type)
    returned = lax.all_to_all(
        result.reshape(received.shape), "expert", split_axis=0, concat_axis=0, tiled=True
    )
    padded_result = jnp.concatenate(
        [returned.reshape(-1, feat_width), jnp.zeros((1, feat_width), half_type)]
    )
    picked = padded_result[slot_index].astype(full_type)
    mixed = middle + jnp.sum(gate_values[:, :, None] * picked, axis=1)
    block_output = mixed.astype(half_type)
    grad_top = cotangent.astype(full_type)
    grad_gate = jnp.sum(grad_top[:, None, :] * picked, axis=2) * kept_float
    pair_grad = (
        (gate_values[:, :, None] * grad_top[:, None, :])
        .astype(half_type)
        .reshape(2 * tok_count, feat_width)
    )
    padded_pair = jnp.concatenate([pair_grad, jnp.zeros((1, feat_width), half_type)])
    grad_result = padded_pair[pair_owner].reshape(expert_count, capacity, feat_width)
    choice_onehot = (
        choices[:, :, None] == jnp.arange(expert_count, dtype=jnp.int32)[None, None, :]
    ).astype(full_type)
    grad_probs = jnp.sum(grad_gate[:, :, None] * choice_onehot, axis=1)
    grad_logits = router_probs * (
        grad_probs - jnp.sum(grad_probs * router_probs, axis=-1, keepdims=True)
    )
    router_grad = dot_full(second_low.T, grad_logits)
    grad_second = dot_full(grad_logits, router.T)
    rows_arrived, grad_arrived = (
        lax.all_to_all(sent, "expert", split_axis=0, concat_axis=0, tiled=True),
        lax.all_to_all(grad_result, "expert", split_axis=0, concat_axis=0, tiled=True),
    )
    block_rows = rows_arrived.reshape(-1, feat_width)
    grad_rows = grad_arrived.reshape(-1, feat_width)
    pre_act = dot_low(block_rows, up_local) + up_bias_local
    act_value, act_pull = jax.vjp(gelu_exact, pre_act)
    act_low = act_value.astype(half_type)
    down_bias_grad = jnp.sum(grad_rows, axis=0, dtype=full_type)
    grad_act = jnp.einsum("rd,fd->rf", grad_rows, down_local, preferred_element_type=full_type)
    grad_pre = act_pull(grad_act)[0].astype(half_type)
    up_bias_grad = jnp.sum(grad_pre, axis=0, dtype=full_type)
    grad_inputs = jnp.einsum(
        "rf,df->rd", grad_pre, up_local, preferred_element_type=full_type
    ).astype(half_type)
    grad_sent = lax.all_to_all(
        grad_inputs.reshape(rows_arrived.shape), "expert", split_axis=0, concat_axis=0, tiled=True
    )
    down_grad = jnp.einsum("rf,rd->fd", act_low, grad_rows, preferred_element_type=full_type)
    up_grad = jnp.einsum("rd,rf->df", block_rows, grad_pre, preferred_element_type=full_type)
    expert_up_grad, expert_up_bias_grad, expert_down_grad, expert_down_bias_grad = (
        lax.psum_scatter(
            up_grad[None].astype(jnp.bfloat16), "dp", scatter_dimension=1, tiled=True
        ).astype(jnp.float32),
        lax.psum_scatter(
            up_bias_grad[None].astype(jnp.bfloat16), "dp", scatter_dimension=1, tiled=True
        ).astype(jnp.float32),
        lax.psum_scatter(
            down_grad[None].astype(jnp.bfloat16), "dp", scatter_dimension=1, tiled=True
        ).astype(jnp.float32),
        lax.psum_scatter(
            down_bias_grad[None].astype(jnp.bfloat16), "dp", scatter_dimension=1, tiled=True
        ).astype(jnp.float32),
    )
    padded_back = jnp.concatenate(
        [grad_sent.reshape(-1, feat_width), jnp.zeros((1, feat_width), half_type)]
    )
    grad_second = grad_second + jnp.sum(padded_back[slot_index].astype(full_type), axis=1)
    grad_norm_two, second_gain_part, second_shift_part = norm_backward(
        grad_second, second_normed, second_inverse, second_gain
    )
    grad_middle = grad_top + grad_norm_two
    grad_branch = grad_middle.astype(half_type)
    out_bias_part = jnp.sum(grad_branch, axis=0, dtype=full_type)
    out_weight_part = jnp.einsum(
        "ti,to->io", attended, grad_branch, preferred_element_type=full_type
    )
    grad_attended = jnp.einsum(
        "to,io->ti", grad_branch, out_weight, preferred_element_type=full_type
    ).astype(half_type)
    grad_att3 = grad_attended.reshape(tok_count, head_count, head_size)
    scores_again = attn_scores(query3, key3, allowed, score_scale)
    probs_again = jnp.exp(scores_again - log_total)
    grad_weights = jnp.einsum("qhd,khd->hqk", grad_att3, value3, preferred_element_type=full_type)
    grad_scores = (
        probs_again * (grad_weights - jnp.sum(grad_weights * probs_again, axis=-1, keepdims=True))
    ).astype(half_type)
    grad_value = (
        jnp.einsum(
            "hqk,qhd->khd",
            probs_again.astype(half_type),
            grad_att3,
            preferred_element_type=full_type,
        )
        .astype(half_type)
        .reshape(tok_count, feat_width)
    )
    grad_query = (
        (
            jnp.einsum("hqk,khd->qhd", grad_scores, key3, preferred_element_type=full_type)
            * score_scale
        )
        .astype(half_type)
        .reshape(tok_count, feat_width)
    )
    grad_key = (
        (
            jnp.einsum("hqk,qhd->khd", grad_scores, query3, preferred_element_type=full_type)
            * score_scale
        )
        .astype(half_type)
        .reshape(tok_count, feat_width)
    )
    query_weight_part = jnp.einsum(
        "ti,to->io", first_low, grad_query, preferred_element_type=full_type
    )
    key_weight_part = jnp.einsum("ti,to->io", first_low, grad_key, preferred_element_type=full_type)
    value_weight_part = jnp.einsum(
        "ti,to->io", first_low, grad_value, preferred_element_type=full_type
    )
    query_bias_part = jnp.sum(grad_query, axis=0, dtype=full_type)
    value_bias_part = jnp.sum(grad_value, axis=0, dtype=full_type)
    grad_first = jnp.einsum("to,io->ti", grad_query, query_weight, preferred_element_type=full_type)
    grad_first = grad_first + jnp.einsum(
        "to,io->ti", grad_key, key_weight, preferred_element_type=full_type
    )
    grad_first = grad_first + jnp.einsum(
        "to,io->ti", grad_value, value_weight, preferred_element_type=full_type
    )
    grad_norm_one, first_gain_part, first_shift_part = norm_backward(
        grad_first, first_normed, first_inverse, first_gain
    )
    input_grad = (grad_middle + grad_norm_one).astype(half_type)
    summed = lax.psum(
        (
            first_gain_part,
            first_shift_part,
            query_weight_part,
            query_bias_part,
            key_weight_part,
            value_weight_part,
            value_bias_part,
            out_weight_part,
            out_bias_part,
            second_gain_part,
            second_shift_part,
            router_grad,
        ),
        ("dp", "expert"),
    )
    return (
        block_output,
        input_grad,
        summed[0],
        summed[1],
        summed[2],
        summed[3],
        summed[4],
        summed[5],
        summed[6],
        summed[7],
        summed[8],
        summed[9],
        summed[10],
        summed[11],
        expert_up_grad,
        expert_up_bias_grad,
        expert_down_grad,
        expert_down_bias_grad,
    )


def solution(mesh):
    return jax.shard_map(
        shards,
        mesh=mesh,
        in_specs=(
            P(("dp", "expert"), None),
            P(),
            P(),
            P(),
            P(),
            P(),
            P(),
            P(),
            P(),
            P(),
            P(),
            P(),
            P(),
            P("expert", None, None),
            P("expert", None),
            P("expert", None, None),
            P("expert", None),
            P(("dp", "expert"), None),
            P(("dp", "expert"), None),
            P(("dp", "expert"), None),
        ),
        out_specs=(
            P(("dp", "expert"), None),
            P(("dp", "expert"), None),
            P(),
            P(),
            P(),
            P(),
            P(),
            P(),
            P(),
            P(),
            P(),
            P(),
            P(),
            P(),
            P("expert", "dp", None),
            P("expert", "dp"),
            P("expert", "dp", None),
            P("expert", "dp"),
        ),
        check_vma=False,
    )
```

profile of v0, /device:TPU:0, one launch (start us, length us, event | category | flops | bytes accessed | tf_op | source)
XLA Modules:
  0.0 920.9 jit_solution(1917073701333418501)
XLA Ops:
  11.2 9.9 %scatter_custom_fusion = s32[1936]{0:T(1024)S(1)} fusion(s32[1936]{0:T(1024)S(1)} %bitcast.151, s32[1936]{0:T(1024)S(1)} %pad_add_fusion, s32[]{:T(128)} %constant.58.clone.1), kind=kCustom, calls=%fused_computation.150 | custom fusion | bytes 7748 | tf_op jit(solution)/shard_map/scatter | solution.py:54
  21.2 2.3 reduce-window.6
  24.1 11.5 %gather_fusion = s32[1936]{0:T(1024)S(1)} fusion(s32[1936]{0:T(1024)S(1)} %fusion.41, s32[2048]{0:T(1024)S(1)} %pad_clamp_fusion.1), kind=kCustom, calls=%fused_computation | custom fusion | bytes 23232 | tf_op jit(solution)/shard_map/gather | solution.py:60
  38.5 9.9 %scatter_custom_fusion.1 = s32[2048]{0:T(1024)S(1)} fusion(s32[1936]{0:T(1024)S(1)} %bitcast.154, s32[1936]{0:T(1024)S(1)} %iota.20, s32[]{:T(128)} %constant.67.clone.1), kind=kCustom, calls=%fused_computation.145 | custom fusion | bytes 8196 | tf_op jit(solution)/shard_map/scatter | solution.py:130
  49.7 4.8 convolution_convert_fusion.5
  54.5 2.7 copy.119
  57.3 4.5 add_convert_fusion.4
  61.7 2.6 copy.118
  64.3 4.1 add_convert_fusion.5
  68.5 2.6 copy.117
  71.0 5.5 mul.220
  76.5 8.0 mul.229
  84.5 20.6 %fusion = (f32[12,968]{1,0:T(8,128)S(1)}, f32[12,968,968]{1,2,0:T(8,128)}) fusion(pred[968,968]{0,1:T(8,128)(4,1)S(1)} %broadcast_compare_fusion, bf16[968,12,64]{0,2,1:T(8,128)(2,1)} %bitcast.126, bf16[968,12,64]{0,2,1:T(8,128)(2,1)} %bitcast.128), kind=kOutput, calls=%fused_computation.14 | convolution fusion | flops 1472990080 | bytes 48934336 | tf_op jit(solution)/shard_map/qhd,khd->hqk/dot_general | solution.py:67
  105.1 20.1 %exponential_reduce_fusion = f32[12,968]{1,0:T(8,128)S(1)} fusion(f32[12,968,968]{1,2,0:T(8,128)} %get-tuple-element.52, f32[12,968]{1,0:T(8,128)S(1)} %get-tuple-element.51, pred[968,968]{0,1:T(8,128)(4,1)S(1)} %broadcast_compare_fusion), kind=kLoop, calls=%fused_computation.11 | loop fusion | flops 44965536 | bytes 46007104 | tf_op jit(solution)/shard_map/reduce_sum | solution.py:113
  125.3 19.7 %convolution_convert_fusion.3 = bf16[12,64,968]{2,1,0:T(8,128)(2,1)S(1)} fusion(bf16[968,12,64]{0,2,1:T(8,128)(2,1)S(1)} %bitcast.133, f32[12,968,968]{1,2,0:T(8,128)} %get-tuple-element.52, f32[12,968]{1,0:T(8,128)S(1)} %log_add_fusion, pred[968,968]{0,1:T(8,128)(4,1)S(1)} %broadcast_compare_fusion), kind=kOutput, calls=%fused_computation.87 | convolution fusion | flops 1484989440 | bytes 48934336 | tf_op jit(solution)/shard_map/hqk,khd->qhd/dot_general | solution.py:116
  150.0 18.5 %gather_fusion.5 = f32[1936]{0:T(1024)S(1)} fusion(f32[968,8]{0,1:T(8,128)S(1)} %fusion.42, s32[1936]{0:T(1024)S(1)} %reshape.435), kind=kCustom, calls=%fused_computation.5 | custom fusion | bytes 30976 | tf_op jit(solution)/shard_map/jit(take_along_axis)/gather | solution.py:126
  169.7 3.1 multiply_convert_fusion.2
  174.6 12.3 %gather_fusion.3 = bf16[2048,768]{1,0:T(8,128)(2,1)} fusion(bf16[1937,768]{1,0:T(8,128)(2,1)} %concatenate.47, s32[2048]{0:T(1024)S(1)} %copy-done.51), kind=kCustom, calls=%fused_computation.3 | custom fusion | bytes 6299648 | tf_op jit(solution)/shard_map/gather | solution.py:161
  186.9 5.2 all-to-all-start.2
  193.6 9.4 %gather_fusion.1 = bf16[2048,768]{1,0:T(8,128)(2,1)} fusion(bf16[969,768]{1,0:T(8,128)(2,1)S(1)} %concatenate.45, s32[2048]{0:T(1024)S(1)} %copy-done.50), kind=kCustom, calls=%fused_computation.1 | custom fusion | bytes 6299648 | tf_op jit(solution)/shard_map/gather | solution.py:134
  202.9 27.1 %all-to-all-done.2 = bf16[8,256,768]{2,1,0:T(8,128)(2,1)} async-done(((bf16[8,256,768]{2,1,0:T(8,128)(2,1)}), bf16[8,256,768]{2,1,0:T(8,128)(2,1)}, u32[]{:S(2)}, u32[]{:S(2)}) %all-to-all-start.2) | async-done | bytes 3145760 | tf_op jit(solution)/shard_map/all_to_all | solution.py:173
  230.1 4.5 all-to-all-start
  234.6 2.4 reduce_sum.271
  237.9 34.5 %all-to-all-done = bf16[8,256,768]{2,1,0:T(8,128)(2,1)} async-done(((bf16[8,256,768]{2,1,0:T(8,128)(2,1)}), bf16[8,256,768]{2,1,0:T(8,128)(2,1)}, u32[]{:S(2)}, u32[]{:S(2)}) %all-to-all-start) | async-done | bytes 3145760 | tf_op jit(solution)/shard_map/all_to_all | solution.py:139
  272.4 65.2 %multiply_convert_fusion.1 = (bf16[2048,3072]{1,0:T(8,128)(2,1)}, f32[2048,3072]{1,0:T(8,128)}, f32[2048,3072]{1,0:T(8,128)}) fusion(f32[3072]{0:T(1024)S(1)} %bitcast.155, bf16[2048,768]{1,0:T(8,128)(2,1)} %bitcast.16, bf16[1,768,3072]{2,1,0:T(8,128)(2,1)} %param.33), kind=kOutput, calls=%fused_computation.17 | convolution fusion | flops 10078912512 | bytes 70791168 | tf_op jit(solution)/shard_map/dot_general | solution.py:18
  337.6 33.2 %fusion.81 = (bf16[3072]{0:T(1024)(128)(2,1)S(1)}, bf16[2048,3072]{1,0:T(8,128)(2,1)}) fusion(f32[2048,3072]{1,0:T(8,128)} %get-tuple-element.45, bf16[2048,768]{1,0:T(8,128)(2,1)} %bitcast.23, bf16[1,3072,768]{2,1,0:T(8,128)(2,1)} %param.35, f32[2048,3072]{1,0:T(8,128)} %get-tuple-element.55, f32[3072]{0:T(1024)S(1)} %bitcast.156), kind=kOutput, calls=%fused_computation.173 | convolution fusion | flops 9764336640 | bytes 70797312 | tf_op jit(solution)/shard_map/rd,fd->rf/dot_general | solution.py:181
  372.2 15.8 %fusion.15 = bf16[1,768,3072]{2,1,0:T(8,128)(2,1)} fusion(bf16[2048,768]{1,0:T(8,128)(2,1)} %bitcast.16, bf16[2048,3072]{1,0:T(8,128)(2,1)} %get-tuple-element.67), kind=kOutput, calls=%fused_computation.45 | convolution fusion | flops 9666035712 | bytes 20447232 | tf_op jit(solution)/shard_map/rd,rf->df/dot_general | solution.py:191
  387.9 15.5 %fusion.25 = bf16[2048,768]{1,0:T(8,128)(2,1)} fusion(bf16[2048,3072]{1,0:T(8,128)(2,1)} %get-tuple-element.67, bf16[1,768,3072]{2,1,0:T(8,128)(2,1)} %param.33), kind=kOutput, calls=%fused_computation.56 | convolution fusion | flops 9665249280 | bytes 20447232 | tf_op jit(solution)/shard_map/rf,df->rd/dot_general | solution.py:184
  403.5 4.6 all-to-all-start.3
  408.1 15.4 %add_convert_fusion.1 = bf16[2048,768]{1,0:T(8,128)(2,1)} fusion(bf16[2048,3072]{1,0:T(8,128)(2,1)} %get-tuple-element.44, bf16[1,3072,768]{2,1,0:T(8,128)(2,1)} %param.35, f32[768]{0:T(1024)S(1)} %reduce.6), kind=kOutput, calls=%fused_computation.32 | convolution fusion | flops 9666822144 | bytes 20450304 | tf_op jit(solution)/shard_map/dot_general | solution.py:18
  423.5 22.5 %all-to-all-done.3 = bf16[8,256,768]{2,1,0:T(8,128)(2,1)} async-done(((bf16[8,256,768]{2,1,0:T(8,128)(2,1)}), bf16[8,256,768]{2,1,0:T(8,128)(2,1)}, u32[]{:S(2)}, u32[]{:S(2)}) %all-to-all-start.3) | async-done | bytes 3145760 | tf_op jit(solution)/shard_map/all_to_all | solution.py:187
  446.0 4.8 all-to-all-start.1
  450.8 1.9 convert_element_type.173
  453.3 15.5 %fusion.16 = bf16[1,3072,768]{2,1,0:T(8,128)(2,1)} fusion(bf16[2048,3072]{1,0:T(8,128)(2,1)} %get-tuple-element.44, bf16[2048,768]{1,0:T(8,128)(2,1)} %bitcast.23), kind=kOutput, calls=%fused_computation.46 | convolution fusion | flops 9666035712 | bytes 20447232 | tf_op jit(solution)/shard_map/rf,rd->fd/dot_general | solution.py:190
  468.8 3.9 concatenate.48
  472.7 15.9 %all-to-all-done.1 = bf16[8,256,768]{2,1,0:T(8,128)(2,1)} async-done(((bf16[8,256,768]{2,1,0:T(8,128)(2,1)}), bf16[8,256,768]{2,1,0:T(8,128)(2,1)}, u32[]{:S(2)}, u32[]{:S(2)}) %all-to-all-start.1) | async-done | bytes 3145760 | tf_op jit(solution)/shard_map/all_to_all | solution.py:144
  488.6 3.8 concatenate.46
  492.4 12.3 %gather_fusion.4 = bf16[1936,768]{1,0:T(8,128)(2,1)} fusion(bf16[2049,768]{1,0:T(8,128)(2,1)} %concatenate.48, s32[2048]{0:T(1024)S(1)} %pad_clamp_fusion), kind=kCustom, calls=%fused_computation.4 | custom fusion | bytes 5955136 | tf_op jit(solution)/shard_map/gather | solution.py:209
  504.7 12.3 %gather_fusion.2 = bf16[1936,768]{1,0:T(8,128)(2,1)} fusion(bf16[2049,768]{1,0:T(8,128)(2,1)} %concatenate.46, s32[2048]{0:T(1024)S(1)} %pad_clamp_fusion), kind=kCustom, calls=%fused_computation.2 | custom fusion | bytes 5955136 | tf_op jit(solution)/shard_map/gather | solution.py:150
  517.1 7.5 reshape.463
  524.6 16.8 %multiply_reduce_fusion.1 = (f32[968,2]{1,0:T(8,128)}, f32[968,768]{1,0:T(8,128)}) fusion(f32[968,2,768]{2,1,0:T(2,128)} %reshape.463, f32[968,768]{1,0:T(8,128)} %convert_element_type.173, f32[968,2]{1,0:T(8,128)S(1)} %copy-done.20), kind=kLoop, calls=%fused_computation.34 | loop fusion | flops 5202032 | bytes 11910272 | tf_op jit(solution)/shard_map/reduce_sum | solution.py:154
  542.7 7.9 reshape.464
  550.7 11.4 %reduce_sum.255 = f32[968,768]{1,0:T(8,128)} reduce(f32[968,2,768]{2,1,0:T(2,128)} %reshape.464, f32[]{:T(128)} %constant.54.clone.1), dimensions={1}, to_apply=%region_17.18 | reduce | flops 743424 | bytes 8921092 | tf_op jit(solution)/shard_map/reduce_sum | solution.py:209
  562.1 5.5 multiply_reduce_fusion.3
  567.7 2.4 convert_reduce_fusion.3
  571.7 2.5 convolution_convert_fusion.4
  574.2 2.8 copy.128
  577.0 20.0 %convert_reduce_fusion.1 = (f32[12,64]{1,0:T(8,128)S(1)}, bf16[12,64,968]{2,1,0:T(8,128)(2,1)}) fusion(bf16[968,12,64]{0,2,1:T(8,128)(2,1)} %bitcast.134, f32[12,968,968]{1,2,0:T(8,128)} %get-tuple-element.52, f32[12,968]{1,0:T(8,128)S(1)} %copy-done.27, pred[968,968]{0,1:T(8,128)(4,1)S(1)} %copy-done.4), kind=kOutput, calls=%fused_computation.57 | convolution fusion | flops 1486475520 | bytes 48937408 | tf_op jit(solution)/shard_map/hqk,qhd->khd/dot_general | solution.py:230
  597.0 33.2 %multiply_reduce_fusion = (f32[12,968]{1,0:T(8,128)S(1)}, f32[12,968,968]{1,2,0:T(8,128)}) fusion(f32[12,968,968]{1,2,0:T(8,128)} %get-tuple-element.52, f32[12,968]{1,0:T(8,128)S(1)} %copy-done.27, pred[968,968]{0,1:T(8,128)(4,1)S(1)} %copy-done.4, bf16[968,12,64]{0,2,1:T(8,128)(2,1)} %bitcast.135, bf16[968,12,64]{0,2,1:T(8,128)(2,1)} %bitcast.132), kind=kOutput, calls=%fused_computation.9 | convolution fusion | flops 1495478656 | bytes 93957952 | tf_op jit(solution)/shard_map/qhd,khd->hqk/dot_general | solution.py:225
  630.3 5.3 fusion.61
  635.6 3.4 fusion.68
  639.0 38.3 %multiply_convert_fusion = bf16[12,968,968]{1,2,0:T(8,128)(2,1)} fusion(f32[12,968,968]{1,2,0:T(8,128)} %get-tuple-element.60, f32[12,968,968]{1,2,0:T(8,128)} %get-tuple-element.52, f32[12,968]{1,0:T(8,128)S(1)} %get-tuple-element.59, f32[12,968]{1,0:T(8,128)S(1)} %copy-done.27, pred[968,968]{0,1:T(8,128)(4,1)S(1)} %copy-done.4), kind=kLoop, calls=%fused_computation.8 | loop fusion | flops 67465728 | bytes 113472832 | tf_op jit(solution)/shard_map/convert_element_type | solution.py:228
  677.3 10.7 %convert_reduce_fusion.2 = (f32[12,64]{1,0:T(8,128)S(1)}, bf16[12,64,968]{2,1,0:T(8,128)(2,1)S(1)}) fusion(bf16[968,12,64]{0,2,1:T(8,128)(2,1)} %bitcast.129, bf16[12,968,968]{1,2,0:T(8,128)(2,1)} %multiply_convert_fusion), kind=kOutput, calls=%fused_computation.58 | convolution fusion | flops 1442241792 | bytes 25465344 | tf_op jit(solution)/shard_map/hqk,khd->qhd/dot_general | solution.py:241
  689.2 3.4 fusion.72
  692.6 12.6 %multiply_convert_fusion.3 = bf16[12,64,968]{2,1,0:T(8,128)(2,1)} fusion(bf16[968,12,64]{0,2,1:T(8,128)(2,1)S(1)} %bitcast.127, bf16[12,968,968]{1,2,0:T(8,128)(2,1)} %multiply_convert_fusion), kind=kOutput, calls=%fused_computation.59 | convolution fusion | flops 1440755712 | bytes 25462272 | tf_op jit(solution)/shard_map/hqk,qhd->khd/dot_general | solution.py:249
  705.2 5.2 fusion.70
  714.6 3.4 fusion.82
  719.9 4.4 fusion.35
  724.3 43.4 %all-reduce.5 = (f32[768]{0:T(1024)}, f32[768]{0:T(1024)}, f32[768]{0:T(1024)}, f32[768]{0:T(1024)}, f32[768]{0:T(1024)}, /*index=5*/f32[768]{0:T(1024)}, f32[768]{0:T(1024)}, f32[768,8]{0,1:T(8,128)}) all-reduce(f32[768]{0:T(1024)S(1)} %get-tuple-element.22, ...), channel_id=1, replica_groups=mesh['dp'=4,'expert'=8] {'dp','expert'}, use_global_device_ids=true, to_apply=%region_24.25 | all-reduce | flops 11520 | bytes 92160 | tf_op jit(solution)/shard_map/psum | solution.py:275
  767.7 4.2 fusion.34
  771.9 2.9 convert_element_type.193
  774.8 2.8 convert_element_type.198
  777.7 126.0 %all-reduce.9.cloned.1.call-done = (f32[768,768]{1,0:T(8,128)}, f32[768,768]{1,0:T(8,128)}, f32[768,768]{1,0:T(8,128)}, f32[768,768]{1,0:T(8,128)}) async-done(((f32[768,768]{1,0:T(8,128)}, f32[768,768]{1,0:T(8,128)}, f32[768,768]{1,0:T(8,128)}, f32[768,768]{1,0:T(8,128)}), (f32[768,768]{1,0:T(8,128)}, f32[768,768]{1,0:T(8,128)}, f32[768,768]{1,0:T(8,128)}, ...) | async-done | bytes 9437200 | tf_op jit(solution)/shard_map/psum | solution.py:275
  903.7 3.4 copy.150
  (226 shorter events, 36.6 us)
Async XLA Ops:
  8.0 56.3 %copy-start = (bf16[768,768]{1,0:T(8,128)(2,1)S(1)}, bf16[768,768]{1,0:T(8,128)(2,1)}, u32[]{:S(2)}) copy-start(bf16[768,768]{1,0:T(8,128)(2,1)} %param.26) | copy-start | bytes 3538948
  24.1 11.6 %copy-start.11 = (bf16[968,768]{1,0:T(8,128)(2,1)S(1)}, bf16[968,768]{1,0:T(8,128)(2,1)}, u32[]{:S(2)}) copy-start(bf16[968,768]{1,0:T(8,128)(2,1)} %param.20) | copy-start | bytes 4460548
  35.7 13.9 %copy-start.55 = (f32[768]{0:T(1024)S(1)}, f32[768]{0:T(1024)}, u32[]{:S(2)}) copy-start(f32[768]{0:T(1024)} %param.21) | copy-start | bytes 9220
  35.7 13.9 %copy-start.65 = (f32[768]{0:T(1024)S(1)}, f32[768]{0:T(1024)}, u32[]{:S(2)}) copy-start(f32[768]{0:T(1024)} %param.22) | copy-start | bytes 9220
  36.0 28.3 %copy-start.45 = (f32[968]{0:T(1024)}, f32[968]{0:T(1024)S(1)}, u32[]{:S(2)}) copy-start(f32[968]{0:T(1024)S(1)} %broadcast_multiply_fusion.5) | copy-start | bytes 11620
  36.6 27.7 %copy-start.52 = (f32[968]{0:T(1024)}, f32[968]{0:T(1024)S(1)}, u32[]{:S(2)}) copy-start(f32[968]{0:T(1024)S(1)} %add_rsqrt_fusion.1) | copy-start | bytes 11620
  36.8 17.7 %copy-start.38 = (pred[2,968]{1,0:T(4,128)(4,1)}, pred[2,968]{1,0:T(4,128)(4,1)S(1)}, u32[]{:S(2)}) copy-start(pred[2,968]{1,0:T(4,128)(4,1)S(1)} %lt.59) | copy-start | bytes 5812
  49.7 75.5 %copy-start.3 = (pred[968,968]{0,1:T(8,128)(4,1)}, pred[968,968]{0,1:T(8,128)(4,1)S(1)}, u32[]{:S(2)}) copy-start(pred[968,968]{0,1:T(8,128)(4,1)S(1)} %broadcast_compare_fusion) | copy-start | bytes 2811076
  54.5 2.7 copy-start.62
  61.7 2.6 copy-start.63
  105.1 20.1 %copy-start.18 = (bf16[968,768]{0,1:T(8,128)(2,1)S(1)}, bf16[968,768]{0,1:T(8,128)(2,1)}, u32[]{:S(2)}) copy-start(bf16[968,768]{0,1:T(8,128)(2,1)} %copy.117) | copy-start | bytes 4460548
  125.2 19.8 %copy-start.26 = (f32[12,968]{1,0:T(8,128)}, f32[12,968]{1,0:T(8,128)S(1)}, u32[]{:S(2)}) copy-start(f32[12,968]{1,0:T(8,128)S(1)} %log_add_fusion) | copy-start | bytes 139396
  125.2 19.8 %copy-start.12 = (bf16[968,768]{1,0:T(8,128)(2,1)S(1)}, bf16[968,768]{1,0:T(8,128)(2,1)}, u32[]{:S(2)}) copy-start(bf16[968,768]{1,0:T(8,128)(2,1)} %param.20) | copy-start | bytes 4460548
  125.2 19.8 %copy-start.58 = (bf16[768,768]{1,0:T(8,128)(2,1)S(1)}, bf16[768,768]{1,0:T(8,128)(2,1)}, u32[]{:S(2)}) copy-start(bf16[768,768]{1,0:T(8,128)(2,1)} %param.28) | copy-start | bytes 3538948
  125.2 19.8 %copy-start.64 = (f32[768]{0:T(1024)S(1)}, f32[768]{0:T(1024)}, u32[]{:S(2)}) copy-start(f32[768]{0:T(1024)} %param.29) | copy-start | bytes 9220
  150.0 18.5 %copy-start.1 = (f32[968,8]{0,1:T(8,128)}, f32[968,8]{0,1:T(8,128)S(1)}, u32[]{:S(2)}) copy-start(f32[968,8]{0,1:T(8,128)S(1)} %fusion.42) | copy-start | bytes 92932
  150.0 19.2 %copy-start.30 = (s32[968,2]{0,1:T(2,128)S(1)}, s32[968,2]{0,1:T(2,128)}, u32[]{:S(2)}) copy-start(s32[968,2]{0,1:T(2,128)} %param.37) | copy-start | bytes 23236
  150.0 19.2 %copy-start.39 = (pred[2,968]{1,0:T(4,128)(4,1)S(1)}, pred[2,968]{1,0:T(4,128)(4,1)}, u32[]{:S(2)}) copy-start(pred[2,968]{1,0:T(4,128)(4,1)} %copy-done.38) | copy-start | bytes 5812
  169.4 3.4 copy-start.19
  172.8 1.8 copy-start.51
  186.9 43.2 %all-to-all-start.2 = ((bf16[8,256,768]{2,1,0:T(8,128)(2,1)}), bf16[8,256,768]{2,1,0:T(8,128)(2,1)}, u32[]{:S(2)}, u32[]{:S(2)}) async-start(bf16[8,256,768]{2,1,0:T(8,128)(2,1)} %bitcast.131), calls=%async_computation.2 | async-start | bytes 6291456 | tf_op jit(solution)/shard_map/all_to_all | solution.py:173
  230.1 42.4 %all-to-all-start = ((bf16[8,256,768]{2,1,0:T(8,128)(2,1)}), bf16[8,256,768]{2,1,0:T(8,128)(2,1)}, u32[]{:S(2)}, u32[]{:S(2)}) async-start(bf16[8,256,768]{2,1,0:T(8,128)(2,1)} %bitcast.130), calls=%async_computation | async-start | bytes 6291456 | tf_op jit(solution)/shard_map/all_to_all | solution.py:139
  234.5 37.9 %copy-start.61 = (f32[1,3072]{1,0:T(1,128)S(1)}, f32[1,3072]{1,0:T(1,128)}, u32[]{:S(2)}) copy-start(f32[1,3072]{1,0:T(1,128)} %param.34) | copy-start | bytes 36868
  234.5 476.0 %reduce-scatter.15.cloned.1.call-start = ((), (), s32[]{:S(2)}) async-start(), calls=%async_computation.11 | async-start | bytes 245760
  237.9 474.2 %reduce-scatter.13.cloned.1.call-start = ((), (), s32[]{:S(2)}) async-start(), calls=%async_computation.10 | async-start | bytes 983040
  372.1 399.8 %reduce-scatter.9.cloned.1.call-start = ((), (), s32[]{:S(2)}) async-start(), calls=%async_computation.8 | async-start | bytes 5898240 | tf_op jit(solution)/shard_map/reduce_scatter | solution.py:193
  403.5 4.6 copy-start.57
  403.5 42.5 %all-to-all-start.3 = ((bf16[8,256,768]{2,1,0:T(8,128)(2,1)}), bf16[8,256,768]{2,1,0:T(8,128)(2,1)}, u32[]{:S(2)}, u32[]{:S(2)}) async-start(bf16[8,256,768]{2,1,0:T(8,128)(2,1)} %bitcast.139), calls=%async_computation.3 | async-start | bytes 6291456 | tf_op jit(solution)/shard_map/all_to_all | solution.py:187
  446.0 4.8 copy-start.10
  446.0 42.7 %all-to-all-start.1 = ((bf16[8,256,768]{2,1,0:T(8,128)(2,1)}), bf16[8,256,768]{2,1,0:T(8,128)(2,1)}, u32[]{:S(2)}, u32[]{:S(2)}) async-start(bf16[8,256,768]{2,1,0:T(8,128)(2,1)} %bitcast.138), calls=%async_computation.1 | async-start | bytes 6291456 | tf_op jit(solution)/shard_map/all_to_all | solution.py:144
  450.8 2.0 copy-start.49
  450.8 324.1 %reduce-scatter.11.cloned.1.call-start = ((), (), s32[]{:S(2)}) async-start(), calls=%async_computation.9 | async-start | bytes 5898240 | tf_op jit(solution)/shard_map/reduce_scatter | solution.py:199
  468.8 434.9 %all-reduce.9.cloned.1.call-start = ((), (), s32[]{:S(2)}) async-start(), calls=%async_computation.12 | async-start | bytes 18874368 | tf_op jit(solution)/shard_map/psum | solution.py:275
  517.1 7.5 copy-start.20
  524.6 18.0 %copy-start.40 = (pred[2,968]{1,0:T(4,128)(4,1)S(1)}, pred[2,968]{1,0:T(4,128)(4,1)}, u32[]{:S(2)}) copy-start(pred[2,968]{1,0:T(4,128)(4,1)} %copy-done.38) | copy-start | bytes 5812
  524.6 18.0 %copy-start.31 = (s32[968,2]{0,1:T(2,128)S(1)}, s32[968,2]{0,1:T(2,128)}, u32[]{:S(2)}) copy-start(s32[968,2]{0,1:T(2,128)} %param.37) | copy-start | bytes 23236
  524.6 18.1 %copy-start.29 = (f32[968,8]{0,1:T(8,128)S(1)}, f32[968,8]{0,1:T(8,128)}, u32[]{:S(2)}) copy-start(f32[968,8]{0,1:T(8,128)} %copy-done.28) | copy-start | bytes 92932
  524.6 18.1 %copy-start.37 = (f32[968]{0:T(1024)S(1)}, f32[968]{0:T(1024)}, u32[]{:S(2)}) copy-start(f32[968]{0:T(1024)} %copy-done.36) | copy-start | bytes 11620
  524.6 18.1 %copy-start.48 = (f32[968]{0:T(1024)S(1)}, f32[968]{0:T(1024)}, u32[]{:S(2)}) copy-start(f32[968]{0:T(1024)} %copy-done.47) | copy-start | bytes 11620
  550.6 11.5 %copy-start.2 = (f32[968,8]{0,1:T(8,128)S(1)}, f32[968,8]{0,1:T(8,128)}, u32[]{:S(2)}) copy-start(f32[968,8]{0,1:T(8,128)} %copy-done.1) | copy-start | bytes 92932
  550.6 11.5 %copy-start.33 = (f32[968]{0:T(1024)S(1)}, f32[968]{0:T(1024)}, u32[]{:S(2)}) copy-start(f32[968]{0:T(1024)} %copy-done.32) | copy-start | bytes 11620
  550.6 11.5 %copy-start.35 = (f32[968]{0:T(1024)S(1)}, f32[968]{0:T(1024)}, u32[]{:S(2)}) copy-start(f32[968]{0:T(1024)} %copy-done.34) | copy-start | bytes 11620
  550.7 11.4 %copy-start.42 = (bf16[768,8]{0,1:T(8,128)(2,1)S(1)}, bf16[768,8]{0,1:T(8,128)(2,1)}, u32[]{:S(2)}) copy-start(bf16[768,8]{0,1:T(8,128)(2,1)} %param.32) | copy-start | bytes 36868
  550.7 11.4 %copy-start.44 = (f32[768]{0:T(1024)S(1)}, f32[768]{0:T(1024)}, u32[]{:S(2)}) copy-start(f32[768]{0:T(1024)} %param.30) | copy-start | bytes 9220
  562.1 5.6 copy-start.6
  562.1 5.6 copy-start.17
  567.7 4.0 copy-start.59
  574.2 2.8 copy-start.4
  574.2 2.8 copy-start.27
  630.3 5.3 copy-start.13
  630.3 5.3 copy-start.46
  630.3 5.3 copy-start.53
  630.3 5.3 copy-start.56
  630.3 5.3 copy-start.66
  630.3 5.3 copy-start.68
  677.3 11.9 %copy-start.14 = (bf16[968,768]{1,0:T(8,128)(2,1)S(1)}, bf16[968,768]{1,0:T(8,128)(2,1)}, u32[]{:S(2)}) copy-start(bf16[968,768]{1,0:T(8,128)(2,1)} %param.20) | copy-start | bytes 4460548
  689.2 3.4 copy-start.7
  710.5 3.4 copy-start.9
  714.5 3.5 copy-start.21
  714.6 3.5 copy-start.60
  718.0 1.9 copy-start.69
  903.7 3.4 copy-start.24
  907.1 2.5 copy-start.23
  909.6 2.5 copy-start.22
  (15 other events, 17.3 us)
Sparse Core Ops, SparseCore 0:
  238.0 21.5 reduce-scatter.14
  372.2 23.3 reduce-scatter.12
  397.9 84.5 reduce-scatter.8
  484.6 85.7 reduce-scatter.10
Sparse Core Ops, SparseCore 1:
  710.6 193.1 all-reduce.8
where the time goes:
time: 929 us; the launch traced here: 921 us
  matrix products  328 us (35%)
  waiting for transfers between devices  226 us (24%)
  local copies, waits for them, and re-layouts  171 us (18%)
  other arithmetic  116 us (12%)
  blocking collectives  43.4 us (5%)
  starting transfers between devices  19.2 us (2%)
  between operations  16.6 us (2%)
    psum x1, waiting for transfers between devices, shards(): lax.psum((first_gain_part, first_shift_part, query_weight_part, query_bia...  126 us
    dot_general x7, matrix products, dot_low(): return jnp.dot(left, right, preferred_element_type=full_type)  96.1 us
    psum x1, blocking collectives, shards(): lax.psum((first_gain_part, first_shift_part, query_weight_part, query_bia...  43.4 us
    convert_element_type x1, other arithmetic, shards(): grad_scores = (probs_again * (grad_weights - jnp.sum(grad_weights * probs...  38.3 us
    all_to_all x1, waiting for transfers between devices, shards(): lax.all_to_all(sent, 'expert', split_axis=0, concat_axis=0, tiled=True)  34.5 us
    dot_general x1, matrix products, shards(): jnp.einsum('qhd,khd->hqk', grad_att3, value3, preferred_element_type=full...  33.2 us
    dot_general x1, matrix products, shards(): jnp.einsum('rd,fd->rf', grad_rows, down_local, preferred_element_type=ful...  33.2 us
    all_to_all x1, waiting for transfers between devices, shards(): lax.all_to_all(grad_result, 'expert', split_axis=0, concat_axis=0, tiled=...  27.1 us
  transfers between devices with their start and end apart: 9, of which 5 were waited for; matrix products, arithmetic and copies ran while one was open for 46% of the time, Pallas kernels for 0%

commit v1 on v0

v1 whole, which is shorter than its diff:
```python
import functools

import jax
import jax.numpy as jnp
from jax import lax
from jax.experimental import pallas as pl
from jax.experimental.pallas import tpu as pltpu
from jax.sharding import PartitionSpec as P

HEADS = 12
BIG = 576
SMALL = 196
LANES = 128
HEAD_GROUPS = 3

half_type = jnp.bfloat16
full_type = jnp.float32
norm_eps = 1e-06
masked_score = -1000000000.0
vmem_bytes = 56 * 2**20


def dot_full(left, right, dims):
    return lax.dot_general(left, right, (dims, ((), ())), preferred_element_type=full_type)


def mul(left, right):
    return dot_full(left, right, ((1,), (0,)))


def mul_t(left, right):
    return dot_full(left, right, ((1,), (1,)))


def t_mul(left, right):
    return dot_full(left, right, ((0,), (0,)))


def row_blocks(rows, step=256):
    return [(start, min(step, rows - start)) for start in range(0, rows, step)]


def iota(shape, dim):
    return lax.broadcasted_iota(jnp.int32, shape, dim)


def ones_where(mask):
    return jnp.where(mask, 1.0, 0.0).astype(half_type)


def normalize(values):
    row_mean = jnp.mean(values, axis=-1, keepdims=True)
    centered = values - row_mean
    inverse = lax.rsqrt(jnp.mean(centered * centered, axis=-1, keepdims=True) + norm_eps)
    return centered * inverse, inverse


def norm_backward(upstream, normed, inverse, norm_gain):
    scaled = upstream * norm_gain
    first_mean = jnp.mean(scaled, axis=-1, keepdims=True)
    second_mean = jnp.mean(scaled * normed, axis=-1, keepdims=True)
    return inverse * (scaled - first_mean - normed * second_mean)


def split_thirds(values, lane, expert_count):
    high = values.astype(half_type).astype(full_type)
    rest = values - high
    middle = rest.astype(half_type).astype(full_type)
    low = rest - middle
    picked = jnp.where(lane < expert_count, high, jnp.where(lane < 2 * expert_count, middle, low))
    return jnp.where(lane < 3 * expert_count, picked, 0.0).astype(half_type)


def call(body, out_shape, name, **kwargs):
    return pl.pallas_call(
        body,
        out_shape=out_shape,
        name=name,
        compiler_params=pltpu.CompilerParams(vmem_limit_bytes=vmem_bytes),
        **kwargs,
    )


def out(shape, dtype):
    return jax.ShapeDtypeStruct(shape, dtype)


def for_experts(expert_count, step):
    if expert_count <= 8:
        for e in range(expert_count):
            step(e)
    else:
        lax.fori_loop(0, expert_count, lambda e, c: (step(e), c)[1], 0)


def expert_rows(e, capacity):
    if isinstance(e, int):
        return pl.ds(e * capacity, capacity)
    return pl.ds(pl.multiple_of(e * capacity, capacity), capacity)


def route_body(expert_count, capacity, cols_ref, rows_ref, rank_col_ref, rank_row_ref, cot_ref, place_ref, slot_ref, sent_ref):
    tok_count = cot_ref.shape[0]
    rank_col, rank_row = rank_col_ref[...], rank_row_ref[...]
    lane = iota((tok_count, LANES), 1)
    first, second = cols_ref[:, 0:1], cols_ref[:, 1:2]
    first_hot, second_hot = ones_where(first == lane), ones_where(second == lane)
    earlier = ones_where(rank_row < rank_col)
    first_total = jnp.sum(first_hot.astype(full_type), axis=0, keepdims=True)
    first_count = mul(earlier, first_hot)
    second_count = mul(earlier, second_hot) + first_total
    first_place = jnp.sum(jnp.where(first == lane, first_count, 0.0), axis=1, keepdims=True).astype(jnp.int32)
    second_place = jnp.sum(jnp.where(second == lane, second_count, 0.0), axis=1, keepdims=True).astype(jnp.int32)
    slot_ref[:, 0:1] = jnp.where(first_place < capacity, first * capacity + first_place, -1)
    slot_ref[:, 1:2] = jnp.where(second_place < capacity, second * capacity + second_place, -1)

    padded = place_ref.shape[0]
    sub = iota((padded, tok_count), 0)
    first, second = rows_ref[0:1, :], rows_ref[1:2, :]
    first_hot, second_hot = ones_where(first == sub), ones_where(second == sub)
    earlier = ones_where(rank_col < rank_row)
    first_total = jnp.sum(first_hot.astype(full_type), axis=1, keepdims=True)
    first_count = mul(first_hot, earlier)
    second_count = mul(second_hot, earlier) + first_total
    place = jnp.where(
        (first == sub) & (first_count < capacity),
        first_count,
        jnp.where((second == sub) & (second_count < capacity), second_count, -1.0),
    )
    place_ref[...] = place.astype(jnp.int32)
    cot = cot_ref[...]
    within = iota((capacity, tok_count), 0)

    def send(e):
        hot = ones_where(place_ref[pl.ds(e, 1), :] == within)
        sent_ref[expert_rows(e, capacity), :] = mul(hot, cot).astype(half_type)

    for_experts(expert_count, send)


def route(choices, priority, cotangent, expert_count, capacity):
    tok_count, feat = cotangent.shape
    padded = -(-expert_count // 32) * 32
    return call(
        functools.partial(route_body, expert_count, capacity),
        (
            out((padded, tok_count), jnp.int32),
            out((tok_count, 2), jnp.int32),
            out((expert_count * capacity, feat), half_type),
        ),
        "route",
    )(choices, choices.T, priority.reshape(tok_count, 1), priority, cotangent)


def image_mask(size):
    key_image = iota((size, 1), 0) // SMALL
    query_image = iota((1, size), 1) // SMALL
    return key_image == query_image


def images(tok_count):
    return ((0, BIG), (BIG, tok_count - BIG))


def head_lanes(value, head):
    lane = iota((1, LANES), 1)
    return jnp.where((lane < LANES // 2) == (head == 0), value, jnp.zeros((), value.dtype))


def front_body(
    expert_count,
    capacity,
    tokens_ref,
    gain_ref,
    shift_ref,
    wq_ref,
    bq_ref,
    wk_ref,
    wv_ref,
    bv_ref,
    wo_ref,
    bo_ref,
    gain2_ref,
    shift2_ref,
    router_ref,
    place_ref,
    first_ref,
    q_ref,
    k_ref,
    v_ref,
    log_big_ref,
    log_small_ref,
    attended_ref,
    middle_ref,
    second_ref,
    probs_ref,
    sent_ref,
    gate_ref,
):
    tok_count, feat = tokens_ref.shape
    scale = (feat // HEADS) ** (-0.5)
    for start, size in row_blocks(tok_count):
        rows = pl.ds(start, size)
        normed, _ = normalize(tokens_ref[rows, :].astype(full_type))
        low = (normed * gain_ref[...] + shift_ref[...]).astype(half_type)
        first_ref[rows, :] = low
        q_ref[rows, :] = (mul(low, wq_ref[...]) + bq_ref[...]).astype(half_type)
        k_ref[rows, :] = mul(low, wk_ref[...]).astype(half_type)
        v_ref[rows, :] = (mul(low, wv_ref[...]) + bv_ref[...]).astype(half_type)

    def pair(number, carry):
        lanes = pl.ds(pl.multiple_of(number * LANES, LANES), LANES)
        for place, (start, size) in enumerate(images(tok_count)):
            rows = pl.ds(start, size)
            query, key, value = q_ref[rows, lanes], k_ref[rows, lanes], v_ref[rows, lanes]
            key = key * jnp.asarray(scale, half_type)
            log_ref = (log_big_ref, log_small_ref)[place]
            value_t = value.T
            halves = []
            for head in range(2):
                scores = mul_t(head_lanes(key, head), query)
                if place:
                    scores = jnp.where(image_mask(size), scores, masked_score)
                top = jnp.max(scores, axis=0, keepdims=True)
                weights = jnp.exp(scores - top)
                total = jnp.sum(weights, axis=0, keepdims=True)
                log_ref[pl.ds(2 * number + head, 1), :] = top + jnp.log(total)
                mixed = mul(value_t[head * 64 : head * 64 + 64], weights.astype(half_type))
                halves.append(mixed * (1.0 / total))
            attended_ref[rows, lanes] = jnp.concatenate(halves, axis=0).T.astype(half_type)
        return carry

    lax.fori_loop(0, HEADS // 2, pair, 0)

    for start, size in row_blocks(tok_count):
        rows = pl.ds(start, size)
        lane = iota((size, LANES), 1)
        middle = tokens_ref[rows, :].astype(full_type) + mul(attended_ref[rows, :], wo_ref[...]) + bo_ref[...]
        middle_ref[rows, :] = middle
        normed, _ = normalize(middle)
        low = (normed * gain2_ref[...] + shift2_ref[...]).astype(half_type)
        second_ref[rows, :] = low
        logits = jnp.where(lane < 3 * expert_count, mul(low, router_ref[...]), masked_score)
        top = jnp.max(logits, axis=1, keepdims=True)
        raised = jnp.exp(logits - top)
        total = jnp.sum(jnp.where(lane < expert_count, raised, 0.0), axis=1, keepdims=True)
        probs_ref[rows, :] = raised / total

    low = second_ref[...]
    lane = iota((tok_count, LANES), 1)
    thirds = split_thirds(probs_ref[...], lane, expert_count)
    within = iota((capacity, tok_count), 0)
    slot_lane = iota((capacity, LANES), 1)

    def send(e):
        hot = ones_where(place_ref[pl.ds(e, 1), :] == within)
        rows = expert_rows(e, capacity)
        sent_ref[rows, :] = mul(hot, low).astype(half_type)
        gates = mul(hot, thirds)
        own = (slot_lane == e) | (slot_lane == e + expert_count) | (slot_lane == e + 2 * expert_count)
        gate_ref[rows, :] = jnp.sum(jnp.where(own, gates, 0.0), axis=1, keepdims=True)

    for_experts(expert_count, send)


def front(tokens, vectors, weights, router3, place, expert_count, capacity):
    tok_count, feat = tokens.shape
    slots = expert_count * capacity
    gain, shift, bq, bv, bo, gain2, shift2 = vectors
    wq, wk, wv, wo = weights
    low = out((tok_count, feat), half_type)
    return call(
        functools.partial(front_body, expert_count, capacity),
        (
            low,
            low,
            low,
            low,
            out((HEADS, BIG), full_type),
            out((HEADS, tok_count - BIG), full_type),
            low,
            out((tok_count, feat), full_type),
            low,
            out((tok_count, LANES), full_type),
            out((slots, feat), half_type),
            out((slots, 1), full_type),
        ),
        "front",
    )(tokens, gain, shift, wq, bq, wk, wv, bv, wo, bo, gain2, shift2, router3, place)


def act_grad_body(cot_ref, gate_ref, down_ref, grad_ref, grad_act_ref, bias_ref):
    @pl.when(pl.program_id(0) == 0)
    def _():
        total = jnp.zeros(bias_ref.shape, full_type)
        for start, size in row_blocks(cot_ref.shape[0]):
            rows = pl.ds(start, size)
            grad = (cot_ref[rows, :].astype(full_type) * gate_ref[rows, :]).astype(half_type)
            grad_ref[rows, :] = grad
            total = total + jnp.sum(grad.astype(full_type), axis=0, keepdims=True)
        bias_ref[...] = total

    for start, size in row_blocks(cot_ref.shape[0]):
        rows = pl.ds(start, size)
        grad_act_ref[rows, :] = mul_t(grad_ref[rows, :], down_ref[...]).astype(half_type)


def act_grad(cot, gate, down, step=512):
    slots, feat = cot.shape
    hidden = down.shape[0]
    return call(
        act_grad_body,
        (out((slots, feat), half_type), out((slots, hidden), half_type), out((1, feat), full_type)),
        "act_grad",
        grid=(hidden // step,),
        in_specs=[
            pl.BlockSpec((slots, feat), lambda f: (0, 0)),
            pl.BlockSpec((slots, 1), lambda f: (0, 0)),
            pl.BlockSpec((step, feat), lambda f: (f, 0)),
        ],
        out_specs=[
            pl.BlockSpec((slots, feat), lambda f: (0, 0)),
            pl.BlockSpec((slots, step), lambda f: (0, f)),
            pl.BlockSpec((1, feat), lambda f: (0, 0)),
        ],
    )(cot, gate, down)


def gelu_parts(values):
    size = jnp.abs(values)
    t = 1.0 / (1.0 + size * (0.3275911 * 0.7071067811865476))
    poly = t * (0.5 * 0.254829592 + t * (0.5 * -0.284496736 + t * (0.5 * 1.421413741 + t * (0.5 * -1.453152027 + t * (0.5 * 1.061405429)))))
    bell = jnp.exp(values * values * -0.5)
    tail = poly * bell
    area = jnp.where(values >= 0.0, 1.0 - tail, tail)
    return values * area, area + values * bell * 0.3989422804014327


def expert_body(rows_ref, up_ref, up_bias_ref, grad_act_ref, act_ref, grad_pre_ref, grad_in_ref, bias_ref, acc_ref):
    step = pl.program_id(0)
    total = jnp.zeros(bias_ref.shape, full_type)

    @pl.when(step == 0)
    def _():
        acc_ref[...] = jnp.zeros(acc_ref.shape, full_type)

    for start, size in row_blocks(rows_ref.shape[0]):
        rows = pl.ds(start, size)
        pre = mul(rows_ref[rows, :], up_ref[...]) + up_bias_ref[...]
        act, slope = gelu_parts(pre)
        act_ref[rows, :] = act.astype(half_type)
        grad_pre = (grad_act_ref[rows, :].astype(full_type) * slope).astype(half_type)
        grad_pre_ref[rows, :] = grad_pre
        total = total + jnp.sum(grad_pre.astype(full_type), axis=0, keepdims=True)
        acc_ref[rows, :] += mul_t(grad_pre, up_ref[...])
    bias_ref[...] = total

    @pl.when(step == pl.num_programs(0) - 1)
    def _():
        grad_in_ref[...] = acc_ref[...].astype(half_type)


def expert(rows, up, up_bias, grad_act, step=512):
    slots, feat = rows.shape
    hidden = up.shape[1]
    wide = pl.BlockSpec((slots, step), lambda f: (0, f))
    return call(
        expert_body,
        (
            out((slots, hidden), half_type),
            out((slots, hidden), half_type),
            out((slots, feat), half_type),
            out((1, hidden), full_type),
        ),
        "expert",
        grid=(hidden // step,),
        in_specs=[
            pl.BlockSpec((slots, feat), lambda f: (0, 0)),
            pl.BlockSpec((feat, step), lambda f: (0, f)),
            pl.BlockSpec((1, step), lambda f: (0, f)),
            wide,
        ],
        out_specs=[
            wide,
            wide,
            pl.BlockSpec((slots, feat), lambda f: (0, 0)),
            pl.BlockSpec((1, step), lambda f: (0, f)),
        ],
        scratch_shapes=[pltpu.VMEM((slots, feat), full_type)],
    )(rows, up, up_bias, grad_act)


def result_body(act_ref, down_ref, down_bias_ref, cot_ref, result_ref, gate_grad_ref):
    result = (mul(act_ref[...], down_ref[...]) + down_bias_ref[...]).astype(half_type)
    result_ref[...] = result
    gate_grad_ref[...] = jnp.sum(result.astype(full_type) * cot_ref[...].astype(full_type), axis=1, keepdims=True)


def expert_result(act, down, down_bias, cot, step=256):
    slots, hidden = act.shape
    feat = down.shape[1]
    narrow = pl.BlockSpec((step, feat), lambda r: (r, 0))
    return call(
        result_body,
        (out((slots, feat), half_type), out((slots, 1), full_type)),
        "result",
        grid=(slots // step,),
        in_specs=[
            pl.BlockSpec((step, hidden), lambda r: (r, 0)),
            pl.BlockSpec((hidden, feat), lambda r: (0, 0)),
            pl.BlockSpec((1, feat), lambda r: (0, 0)),
            narrow,
        ],
        out_specs=[narrow, pl.BlockSpec((step, 1), lambda r: (r, 0))],
    )(act, down, down_bias, cot)


def combine_body(
    expert_count,
    capacity,
    back_ref,
    gate_grad_ref,
    slot_ref,
    probs_ref,
    middle_ref,
    cot_ref,
    attended_ref,
    wo_ref,
    router_ref,
    gain_ref,
    shift_ref,
    grad_middle_ref,
    grad_attended_ref,
    wo_grad_ref,
    router_grad_ref,
    vector_ref,
):
    tok_count, feat = cot_ref.shape
    slots = back_ref.shape[0]
    owner = iota((slots, LANES), 0) // capacity
    lane = iota((slots, LANES), 1)
    same = (lane == owner) | (lane == owner + expert_count) | (lane == owner + 2 * expert_count)
    gate_table = split_thirds(jnp.where(same, gate_grad_ref[...], 0.0), lane, expert_count)
    wo_grad = jnp.zeros(wo_grad_ref.shape, full_type)
    router_grad = jnp.zeros(router_grad_ref.shape, full_type)
    gain_grad = jnp.zeros((1, feat), full_type)
    shift_grad = jnp.zeros((1, feat), full_type)
    bias_grad = jnp.zeros((1, feat), full_type)
    for start, size in row_blocks(tok_count):
        rows = pl.ds(start, size)
        number = iota((size, slots), 1)
        hot = ones_where((number == slot_ref[rows, 0:1]) | (number == slot_ref[rows, 1:2]))
        lane = iota((size, LANES), 1)
        folded = mul(hot, gate_table)
        folded = folded + pltpu.roll(folded, LANES - expert_count, 1) + pltpu.roll(folded, LANES - 2 * expert_count, 1)
        probs = jnp.where(lane < expert_count, probs_ref[rows, :], 0.0)
        grad_probs = jnp.where(lane < expert_count, folded, 0.0)
        grad_logits = probs * (grad_probs - jnp.sum(grad_probs * probs, axis=1, keepdims=True))
        grad_logits = grad_logits + pltpu.roll(grad_logits, expert_count, 1) + pltpu.roll(grad_logits, 2 * expert_count, 1)
        thirds = split_thirds(grad_logits, lane, expert_count)
        upstream = mul_t(thirds, router_ref[...]) + mul(hot, back_ref[...])
        normed, inverse = normalize(middle_ref[rows, :])
        low = (normed * gain_ref[...] + shift_ref[...]).astype(half_type)
        router_grad = router_grad + t_mul(low, thirds)
        gain_grad = gain_grad + jnp.sum(upstream * normed, axis=0, keepdims=True)
        shift_grad = shift_grad + jnp.sum(upstream, axis=0, keepdims=True)
        grad_middle = cot_ref[rows, :].astype(full_type) + norm_backward(upstream, normed, inverse, gain_ref[...])
        grad_middle_ref[rows, :] = grad_middle
        branch = grad_middle.astype(half_type)
        bias_grad = bias_grad + jnp.sum(branch.astype(full_type), axis=0, keepdims=True)
        grad_attended_ref[rows, :] = mul_t(branch, wo_ref[...]).astype(half_type)
        wo_grad = wo_grad + t_mul(attended_ref[rows, :], branch)
    wo_grad_ref[...] = wo_grad.astype(half_type)
    router_grad = router_grad + pltpu.roll(router_grad, LANES - expert_count, 1) + pltpu.roll(router_grad, LANES - 2 * expert_count, 1)
    router_grad_ref[...] = router_grad
    vector_ref[0:1, :] = gain_grad
    vector_ref[1:2, :] = shift_grad
    vector_ref[2:3, :] = bias_grad


def combine(back, gate_grad, slot, probs, middle, cot, attended, wo, router3, gain, shift, expert_count, capacity):
    tok_count, feat = cot.shape
    return call(
        functools.partial(combine_body, expert_count, capacity),
        (
            out((tok_count, feat), full_type),
            out((tok_count, feat), half_type),
            out((feat, feat), half_type),
            out((feat, LANES), full_type),
            out((3, feat), full_type),
        ),
        "combine",
    )(back, gate_grad, slot, probs, middle, cot, attended, wo, router3, gain, shift)


def attention_grad_body(first_head, q_ref, k_ref, v_ref, grad_ref, log_big_ref, log_small_ref, first_ref, dq_ref, dk_ref, dv_ref, wq_ref, wk_ref, wv_ref, bias_ref):
    tok_count, width = q_ref.shape
    scale = 64 ** (-0.5)

    def pair(number, carry):
        lanes = pl.ds(pl.multiple_of(number * LANES, LANES), LANES)
        for place, (start, size) in enumerate(images(tok_count)):
            rows = pl.ds(start, size)
            query, key, value, grad = q_ref[rows, lanes], k_ref[rows, lanes], v_ref[rows, lanes], grad_ref[rows, lanes]
            key = key * jnp.asarray(scale, half_type)
            log_ref = (log_big_ref, log_small_ref)[place]
            key_t = key.T
            halves = []
            grad_value = jnp.zeros((size, LANES), full_type)
            grad_key = jnp.zeros((size, LANES), full_type)
            for head in range(2):
                scores = mul_t(head_lanes(key, head), query)
                if place:
                    scores = jnp.where(image_mask(size), scores, masked_score)
                probs = jnp.exp(scores - log_ref[pl.ds(first_head + 2 * number + head, 1), :])
                grad_probs = mul_t(head_lanes(value, head), grad)
                inner = jnp.sum(grad_probs * probs, axis=0, keepdims=True)
                grad_scores = (probs * (grad_probs - inner)).astype(half_type)
                grad_value = grad_value + mul(probs.astype(half_type), head_lanes(grad, head))
                grad_key = grad_key + mul(grad_scores, head_lanes(query, head))
                halves.append(mul(key_t[head * 64 : head * 64 + 64], grad_scores))
            dv_ref[rows, lanes] = grad_value.astype(half_type)
            dk_ref[rows, lanes] = (grad_key * scale).astype(half_type)
            dq_ref[rows, lanes] = jnp.concatenate(halves, axis=0).T.astype(half_type)
        return carry

    lax.fori_loop(0, width // LANES, pair, 0)
    first = first_ref[...]
    wq_ref[...] = t_mul(first, dq_ref[...]).astype(half_type)
    wk_ref[...] = t_mul(first, dk_ref[...]).astype(half_type)
    wv_ref[...] = t_mul(first, dv_ref[...]).astype(half_type)
    bias_ref[0:1, :] = jnp.sum(dq_ref[...].astype(full_type), axis=0, keepdims=True)
    bias_ref[1:2, :] = jnp.sum(dv_ref[...].astype(full_type), axis=0, keepdims=True)


def attention_grad(group, q, k, v, grad, log_big, log_small, first):
    tok_count, feat = q.shape
    width = feat // HEAD_GROUPS
    columns = pl.BlockSpec((tok_count, width), lambda i: (0, group))
    whole = lambda a: pl.BlockSpec(a.shape, lambda i: (0, 0))
    low = out((tok_count, width), half_type)
    grads = out((feat, width), half_type)
    return call(
        functools.partial(attention_grad_body, group * HEADS // HEAD_GROUPS),
        (low, low, low, grads, grads, grads, out((2, width), full_type)),
        f"attention_grad_{group}",
        grid=(1,),
        in_specs=[columns, columns, columns, columns, whole(log_big), whole(log_small), whole(first)],
    )(q, k, v, grad, log_big, log_small, first)


def input_grad_body(*refs):
    grads = refs[: 3 * HEAD_GROUPS]
    wq_ref, wk_ref, wv_ref, tokens_ref, gain_ref, middle_ref, result_ref, vector_ref = refs[3 * HEAD_GROUPS :]
    tok_count, feat = tokens_ref.shape
    width = feat // HEAD_GROUPS
    gain_grad = jnp.zeros((1, feat), full_type)
    shift_grad = jnp.zeros((1, feat), full_type)
    for start, size in row_blocks(tok_count):
        rows = pl.ds(start, size)
        upstream = jnp.zeros((size, feat), full_type)
        for group in range(HEAD_GROUPS):
            lanes = pl.ds(group * width, width)
            for grad_ref, weight_ref in zip(grads[3 * group : 3 * group + 3], (wq_ref, wk_ref, wv_ref)):
                upstream = upstream + mul_t(grad_ref[rows, :], weight_ref[:, lanes])
        normed, inverse = normalize(tokens_ref[rows, :].astype(full_type))
        gain_grad = gain_grad + jnp.sum(upstream * normed, axis=0, keepdims=True)
        shift_grad = shift_grad + jnp.sum(upstream, axis=0, keepdims=True)
        grad = middle_ref[rows, :] + norm_backward(upstream, normed, inverse, gain_ref[...])
        result_ref[rows, :] = grad.astype(half_type)
    vector_ref[0:1, :] = gain_grad
    vector_ref[1:2, :] = shift_grad


def input_grad(grads, wq, wk, wv, tokens, gain, grad_middle):
    tok_count, feat = tokens.shape
    return call(
        input_grad_body,
        (out((tok_count, feat), half_type), out((2, feat), full_type)),
        "input_grad",
    )(*grads, wq, wk, wv, tokens, gain, grad_middle)


def output_body(returned_ref, slot_ref, choice_ref, probs_ref, middle_ref, result_ref):
    tok_count, feat = middle_ref.shape
    slots = returned_ref.shape[0]
    for start, size in row_blocks(tok_count):
        rows = pl.ds(start, size)
        lane = iota((size, LANES), 1)
        number = iota((size, slots), 1)
        probs = probs_ref[rows, :]
        table = jnp.zeros((size, slots), full_type)
        for k in range(2):
            gate = jnp.sum(jnp.where(lane == choice_ref[rows, k : k + 1], probs, 0.0), axis=1, keepdims=True)
            table = jnp.where(number == slot_ref[rows, k : k + 1], gate, table)
        high = table.astype(half_type)
        low = (table - high.astype(full_type)).astype(half_type)
        mixed = mul(high, returned_ref[...]) + mul(low, returned_ref[...])
        result_ref[rows, :] = (middle_ref[rows, :] + mixed).astype(half_type)


def block_result(returned, slot, choices, probs, middle):
    return call(output_body, out(middle.shape, half_type), "block_result")(returned, slot, choices, probs, middle)


def exchange(values, expert_count):
    split = values.reshape(expert_count, -1, values.shape[1])
    swapped = lax.all_to_all(split, "expert", split_axis=0, concat_axis=0, tiled=True)
    return swapped.reshape(values.shape)


def exchange_column(values, expert_count):
    split = values.reshape(expert_count, -1)
    return lax.all_to_all(split, "expert", split_axis=0, concat_axis=0, tiled=True).reshape(values.shape)


def scatter_sum(values):
    return lax.psum_scatter(values[None], "dp", scatter_dimension=1, tiled=True).astype(full_type)


def shards(
    tokens,
    first_gain,
    first_shift,
    query_weight,
    query_bias,
    key_weight,
    value_weight,
    value_bias,
    out_weight,
    out_bias,
    second_gain,
    second_shift,
    router,
    expert_up,
    expert_up_bias,
    expert_down,
    expert_down_bias,
    choices,
    priority,
    cotangent,
):
    tok_count, feat = tokens.shape
    expert_count = lax.axis_size("expert")
    capacity = (21 * tok_count + 80 * expert_count - 1) // (80 * expert_count) * 8
    row = lambda v: v.reshape(1, -1)
    gain, shift, gain2, shift2 = row(first_gain), row(first_shift), row(second_gain), row(second_shift)
    router3 = jnp.pad(jnp.concatenate([router] * 3, axis=1), ((0, 0), (0, LANES - 3 * expert_count)))
    up, down = expert_up[0], expert_down[0]

    place, slot, cot_sent = route(choices, priority, cotangent, expert_count, capacity)
    cot_rows = exchange(cot_sent, expert_count)
    first, q, k, v, log_big, log_small, attended, middle, _, probs, sent, gate = front(
        tokens,
        (gain, shift, row(query_bias), row(value_bias), row(out_bias), gain2, shift2),
        (query_weight, key_weight, value_weight, out_weight),
        router3,
        place,
        expert_count,
        capacity,
    )
    gate_rows = exchange_column(gate, expert_count)
    arrived = exchange(sent, expert_count)
    grad_rows, grad_act, down_bias_part = act_grad(cot_rows, gate_rows, down)
    act, grad_pre, grad_in, up_bias_part = expert(arrived, up, row(expert_up_bias), grad_act)
    back = exchange(grad_in, expert_count)
    down_grad = t_mul(act, grad_rows).astype(half_type)
    expert_down_grad = scatter_sum(down_grad)
    result, gate_grad = expert_result(act, down, row(expert_down_bias), cot_rows)
    gate_grad_back = exchange_column(gate_grad, expert_count)
    returned = exchange(result, expert_count)
    up_grad = t_mul(arrived, grad_pre).astype(half_type)
    expert_up_grad = scatter_sum(up_grad)
    expert_up_bias_grad = scatter_sum(up_bias_part.reshape(-1).astype(half_type))
    expert_down_bias_grad = scatter_sum(down_bias_part.reshape(-1).astype(half_type))

    grad_middle, grad_attended, wo_grad, router_part, second_parts = combine(
        back, gate_grad_back, slot, probs, middle, cotangent, attended, out_weight, router3, gain2, shift2, expert_count, capacity
    )
    both = ("dp", "expert")
    out_weight_grad = lax.psum(wo_grad, both).astype(full_type)
    grads, bias_parts, weight_parts = [], [], []
    for group in range(HEAD_GROUPS):
        dq, dk, dv, wq_part, wk_part, wv_part, bias_part = attention_grad(
            group, q, k, v, grad_attended, log_big, log_small, first
        )
        grads += [dq, dk, dv]
        bias_parts.append(bias_part)
        weight_parts.append(lax.psum(jnp.stack([wq_part, wk_part, wv_part]), both))
    weight_grads = jnp.concatenate(weight_parts, axis=2).astype(full_type)
    bias_part = jnp.concatenate(bias_parts, axis=1)
    token_grad, first_parts = input_grad(grads, query_weight, key_weight, value_weight, tokens, gain, grad_middle)
    block_output = block_result(returned, slot, choices, probs, middle)
    vectors, router_grad = lax.psum(
        (jnp.concatenate([first_parts, bias_part, second_parts]), router_part[:, :expert_count]), both
    )
    return (
        block_output,
        token_grad,
        vectors[0],
        vectors[1],
        weight_grads[0],
        vectors[2],
        weight_grads[1],
        weight_grads[2],
        vectors[3],
        out_weight_grad,
        vectors[6],
        vectors[4],
        vectors[5],
        router_grad,
        expert_up_grad,
        expert_up_bias_grad,
        expert_down_grad,
        expert_down_bias_grad,
    )


def solution(mesh):
    tokens_spec = P(("dp", "expert"), None)
    return jax.shard_map(
        shards,
        mesh=mesh,
        in_specs=(tokens_spec,)
        + (P(),) * 12
        + (P("expert", None, None), P("expert", None), P("expert", None, None), P("expert", None))
        + (tokens_spec,) * 3,
        out_specs=(tokens_spec,) * 2
        + (P(),) * 12
        + (P("expert", "dp", None), P("expert", "dp"), P("expert", "dp", None), P("expert", "dp")),
        check_vma=False,
    )
```

time: 929 us -> 643 us (0.69)
  matrix products: 328 us -> 29.1 us
  Pallas kernels: 0 us -> 194 us
  local copies, waits for them, and re-layouts: 171 us -> 33.1 us
  other arithmetic: 116 us -> 19.4 us
  blocking collectives: 43.4 us -> 109 us
    dot_general x27 -> x2, matrix products: 328 us -> 29.1 us  [dot_full(): lax.dot_general(left, right, (dims, ((), ())), preferred_element_type=ful...]
    pallas_call x0 -> x11, Pallas kernels: none -> 194 us  [the longest x1 47.4 us: expert(): call(expert_body, (out((slots, hidden), half_type), out((slots, hidden),...]
    gather x10 -> x0, local copies, waits for them, and re-layouts: 77.4 us -> none  [the longest x5 19.6 us: shards(): jnp.take_along_axis(router_probs, choices, axis=1) * kept_float]
    all_to_all x0 -> x3, blocking collectives: none -> 57.8 us  [the longest x1 41 us: exchange(): lax.all_to_all(split, 'expert', split_axis=0, concat_axis=0, tiled=True)]
    reduce_sum x12 -> x0, other arithmetic: 54.4 us -> none  [the longest x1 20.1 us: shards(): jnp.sum(jnp.exp(scores - row_max), axis=-1, keepdims=True)]
    convert_element_type x9 -> x8, other arithmetic: 54.9 us -> 10.6 us  [the longest x4 6.98 us: scatter_sum(): lax.psum_scatter(values[None], 'dp', scatter_dimension=1, tiled=True)]
    convert_element_type x6 -> x0, local copies, waits for them, and re-layouts: 26.1 us -> none  [the longest x1 7.88 us: shards(): padded_back[slot_index].astype(full_type)]
    scatter x2 -> x0, local copies, waits for them, and re-layouts: 19.9 us -> none  [the longest x1 9.94 us: shards(): pair_owner = jnp.full((slot_total,), 2 * tok_count, jnp.int32).at[slot_in...]
  transfers between devices with their start and end apart: 9 -> 8, of which waited for: 5 -> 4; matrix products, arithmetic and copies ran while one was open for 46% -> 8% of each run, Pallas kernels for 0% -> 14%
where the time goes in v1:
time: 643 us; the launch traced here: 633 us
  waiting for transfers between devices  220 us (34%)
  Pallas kernels  194 us (30%)
  blocking collectives  109 us (17%)
  local copies, waits for them, and re-layouts  33.1 us (5%)
  matrix products  29.1 us (5%)
  other arithmetic  19.4 us (3%)
  between operations  15.7 us (2%)
  starting transfers between devices  12.1 us (2%)
    psum x1, waiting for transfers between devices, shards(): weight_parts.append(lax.psum(jnp.stack([wq_part, wk_part, wv_part]), both))  131 us
    all_to_all x3, waiting for transfers between devices, exchange(): lax.all_to_all(split, 'expert', split_axis=0, concat_axis=0, tiled=True)  88.9 us
    psum x1, blocking collectives, shards(): lax.psum((jnp.concatenate([first_parts, bias_part, second_parts]), router...  51.2 us
    pallas_call x1, Pallas kernels, expert(): call(expert_body, (out((slots, hidden), half_type), out((slots, hidden),...  47.4 us
    all_to_all x1, blocking collectives, exchange(): lax.all_to_all(split, 'expert', split_axis=0, concat_axis=0, tiled=True)  41 us
    pallas_call x3, Pallas kernels, attention_grad(): call(functools.partial(attention_grad_body, group * HEADS // HEAD_GROUPS)...  36.3 us
    pallas_call x1, Pallas kernels, front(): call(functools.partial(front_body, expert_count, capacity), (low, low, lo...  30.3 us
    dot_general x2, matrix products, dot_full(): lax.dot_general(left, right, (dims, ((), ())), preferred_element_type=ful...  29.1 us
  transfers between devices with their start and end apart: 8, of which 4 were waited for; matrix products, arithmetic and copies ran while one was open for 8% of the time, Pallas kernels for 14%

profile of v1, /device:TPU:0, one launch (start us, length us, event | category | flops | bytes accessed | tf_op | source)
XLA Modules:
  0.0 633.2 jit_solution(2375518397559848053)
XLA Ops:
  8.0 1.3 reshape.102.gain_ref.refs_13_
  9.3 1.3 reshape.107.gain2_ref.gain_ref
  10.6 1.3 reshape.108.shift2_ref.shift_ref
  11.8 1.3 reshape.103.shift_ref
  13.1 1.3 reshape.104.bq_ref
  14.4 1.3 reshape.105.bv_ref
  15.6 1.3 reshape.106.bo_ref
  16.9 0.8 pad_maximum_fusion.3
  17.7 0.2 copy.53
  17.9 1.7 copy.54.cols_ref.choice_ref
  19.6 1.7 copy.55.rank_col_ref
  21.3 0.7 pad.4.router_ref
  22.0 9.0 %route.1 = (s32[32,968]{1,0:T(8,128)}, s32[968,2]{1,0:T(8,128)}, bf16[2048,768]{1,0:T(8,128)(2,1)}) custom-call(s32[968,2]{1,0:T(8,128)} %copy.54.cols_ref.choice_ref, s32[2,968]{1,0:T(2,128)} %bitcast.71, s32[968,1]{1,0:T(8,128)} %copy.55.rank_col_ref, s32[1,968]{1,0:T(1,128)} %rank_row_ref.1, bf16[968,768]{1,0:T(8,128)(2,1)} %cot_ref.3), custom_call_target="tpu_custom_call" | custom-call | tf_op jit(solution)/shard_map/route/pallas_call | solution.py:144
  31.0 30.3 %front.1 = (bf16[968,768]{1,0:T(8,128)(2,1)}, bf16[968,768]{1,0:T(8,128)(2,1)}, bf16[968,768]{1,0:T(8,128)(2,1)}, bf16[968,768]{1,0:T(8,128)(2,1)}, f32[12,576]{...) custom-call(bf16[968,768]{1,0:T(8,128)(2,1)} %refs_12_.1, ...), custom_call_target="tpu_custom_call" | custom-call | tf_op jit(solution)/shard_map/front/pallas_call | solution.py:272
  61.3 1.6 reduce
  62.9 9.7 %all_to_all.40 = f32[8,1,256]{2,1,0:T(1,128)S(1)} all-to-all(f32[8,1,256]{2,1,0:T(1,128)S(1)} %bitcast.75), channel_id=1, replica_groups=mesh['dp'=4,'expert'=8] {'expert'}, dimensions={0} | all-to-all | bytes 16384 | tf_op jit(solution)/shard_map/all_to_all | solution.py:614
  72.6 41.0 %all_to_all.41 = bf16[8,256,768]{2,1,0:T(8,128)(2,1)} all-to-all(bf16[8,256,768]{2,1,0:T(8,128)(2,1)S(1)} %bitcast.56), channel_id=1, replica_groups=mesh['dp'=4,'expert'=8] {'expert'}, dimensions={0} | all-to-all | bytes 6291456 | tf_op jit(solution)/shard_map/all_to_all | solution.py:608
  113.6 4.1 all-to-all-start
  117.7 1.3 copy.57.gate_ref
  119.0 16.1 %act_grad.1 = (bf16[2048,768]{1,0:T(8,128)(2,1)}, bf16[2048,3072]{1,0:T(8,128)(2,1)}, f32[1,768]{1,0:T(1,128)}) custom-call(bf16[2048,768]{1,0:T(8,128)(2,1)} %bitcast.44, f32[2048,1]{1,0:T(8,128)} %copy.57.gate_ref, bf16[3072,768]{1,0:T(8,128)(2,1)} %bitcast.46), custom_call_target="tpu_custom_call" | custom-call | tf_op jit(solution)/shard_map/act_grad/pallas_call | solution.py:311
  135.1 20.4 %all-to-all-done = bf16[8,256,768]{2,1,0:T(8,128)(2,1)S(1)} async-done(((bf16[8,256,768]{2,1,0:T(8,128)(2,1)}), bf16[8,256,768]{2,1,0:T(8,128)(2,1)S(1)}, u32[]{:S(2)}, u32[]{:S(2)}) %all-to-all-start) | async-done | bytes 3145760 | tf_op jit(solution)/shard_map/all_to_all | solution.py:608
  155.5 1.6 copy-done.2
  157.1 47.4 %expert.1 = (bf16[2048,3072]{1,0:T(8,128)(2,1)}, bf16[2048,3072]{1,0:T(8,128)(2,1)}, bf16[2048,768]{1,0:T(8,128)(2,1)}, f32[1,3072]{1,0:T(1,128)}) custom-call(bf16[2048,768]{1,0:T(8,128)(2,1)} %bitcast.50, bf16[768,3072]{1,0:T(8,128)(2,1)} %bitcast.52, f32[1,3072]{1,0:T(1,128)} %up_bias_ref.1, bf16[2048,3072]{1,0:T(8,128)(2,1)} %get-tuple-element.73.grad_act_ref), custom_call_target="tpu_custom_call" | custom-call | tf_op jit(solution)/shard_map/expert/pallas_call | solution.py:367
  204.5 16.0 %result.1 = (bf16[2048,768]{1,0:T(8,128)(2,1)}, f32[2048,1]{1,0:T(8,128)}) custom-call(bf16[2048,3072]{1,0:T(8,128)(2,1)} %get-tuple-element.74.act_ref, bf16[3072,768]{1,0:T(8,128)(2,1)} %bitcast.47, f32[1,768]{1,0:T(1,128)} %down_bias_ref.1, bf16[2048,768]{1,0:T(8,128)(2,1)} %bitcast.45), custom_call_target="tpu_custom_call" | custom-call | tf_op jit(solution)/shard_map/result/pallas_call | solution.py:403
  220.5 1.6 reduce.1
  222.1 7.1 %all_to_all.42 = f32[8,1,256]{2,1,0:T(1,128)S(1)} all-to-all(f32[8,1,256]{2,1,0:T(1,128)S(1)} %bitcast.74), channel_id=1, replica_groups=mesh['dp'=4,'expert'=8] {'expert'}, dimensions={0} | all-to-all | bytes 16384 | tf_op jit(solution)/shard_map/all_to_all | solution.py:614
  229.2 3.8 all-to-all-start.4
  232.9 0.0 reduce-scatter.15.cloned.1.call-start
  233.0 0.8 copy.64
  234.0 1.3 copy.62
  235.3 0.2 all-reduce.5.cloned.1.call-start
  235.5 1.3 copy.60.gate_grad_ref
  236.8 33.9 %all-to-all-done.4 = bf16[8,256,768]{2,1,0:T(8,128)(2,1)S(1)} async-done(((bf16[8,256,768]{2,1,0:T(8,128)(2,1)}), bf16[8,256,768]{2,1,0:T(8,128)(2,1)S(1)}, u32[]{:S(2)}, u32[]{:S(2)}) %all-to-all-start.4) | async-done | bytes 3145760 | tf_op jit(solution)/shard_map/all_to_all | solution.py:608
  270.8 1.7 copy-done.1
  272.5 16.5 %combine.1 = (f32[968,768]{1,0:T(8,128)}, bf16[968,768]{1,0:T(8,128)(2,1)}, bf16[768,768]{1,0:T(8,128)(2,1)}, f32[768,128]{1,0:T(8,128)}, f32[3,768]{1,0:T(4,128)}) custom-call(bf16[2048,768]{1,0:T(8,128)(2,1)} %bitcast.49, f32[2048,1]{1,0:T(8,128)} %copy.60.gate_grad_ref, s32[968,2]{1,0:T(8,128)} %get-tuple-element.76.slot_ref, ...), custom_call_target="tpu_custom_call" | custom-call | tf_op jit(solution)/shard_map/combine/pallas_call | solution.py:483
  289.0 12.0 %attention_grad_2.1 = (bf16[968,256]{1,0:T(8,128)(2,1)}, bf16[968,256]{1,0:T(8,128)(2,1)}, bf16[968,256]{1,0:T(8,128)(2,1)}, bf16[768,256]{1,0:T(8,128)(2,1)}, b...) custom-call(bf16[968,768]{1,0:T(8,128)(2,1)} %get-tuple-element.79.q_ref, ...), custom_call_target="tpu_custom_call" | custom-call | tf_op jit(solution)/shard_map/attention_grad_2/pallas_call | solution.py:543
  301.0 11.9 %attention_grad_1.1 = (bf16[968,256]{1,0:T(8,128)(2,1)}, bf16[968,256]{1,0:T(8,128)(2,1)}, bf16[968,256]{1,0:T(8,128)(2,1)}, bf16[768,256]{1,0:T(8,128)(2,1)}, b...) custom-call(bf16[968,768]{1,0:T(8,128)(2,1)} %get-tuple-element.79.q_ref, ...), custom_call_target="tpu_custom_call" | custom-call | tf_op jit(solution)/shard_map/attention_grad_1/pallas_call | solution.py:543
  313.0 12.3 %attention_grad_0.1 = (bf16[968,256]{1,0:T(8,128)(2,1)}, bf16[968,256]{1,0:T(8,128)(2,1)}, bf16[968,256]{1,0:T(8,128)(2,1)}, bf16[768,256]{1,0:T(8,128)(2,1)}, b...) custom-call(bf16[968,768]{1,0:T(8,128)(2,1)} %get-tuple-element.79.q_ref, ...), custom_call_target="tpu_custom_call" | custom-call | tf_op jit(solution)/shard_map/attention_grad_0/pallas_call | solution.py:543
  325.3 3.0 pad_maximum_fusion
  328.3 1.1 pad_maximum_fusion.2
  329.5 0.0 reduce-scatter.11.cloned.1.call-start
  329.6 1.8 copy-done.21
  331.4 14.6 %fusion.1 = bf16[1,3072,768]{2,1,0:T(8,128)(2,1)} fusion(bf16[2048,3072]{1,0:T(8,128)(2,1)} %get-tuple-element.74.act_ref, bf16[2048,768]{1,0:T(8,128)(2,1)S(1)} %copy-done.21), kind=kOutput, calls=%fused_computation.3 | convolution fusion | flops 9666035712 | bytes 20447232 | tf_op jit(solution)/shard_map/dot_general | solution.py:24
  346.0 1.9 copy-done.3
  347.9 14.5 %fusion = bf16[1,768,3072]{2,1,0:T(8,128)(2,1)} fusion(bf16[2048,768]{1,0:T(8,128)(2,1)S(1)} %bitcast.51, bf16[2048,3072]{1,0:T(8,128)(2,1)} %get-tuple-element.116), kind=kOutput, calls=%fused_computation.2 | convolution fusion | flops 9666035712 | bytes 20447232 | tf_op jit(solution)/shard_map/dot_general | solution.py:24
  362.4 3.8 all-to-all-start.3
  366.3 0.9 copy.65
  367.2 0.6 convert_element_type.43
  367.8 1.0 copy.63
  368.8 0.6 convert_element_type.39
  369.4 34.7 %all-to-all-done.3 = bf16[8,256,768]{2,1,0:T(8,128)(2,1)S(1)} async-done(((bf16[8,256,768]{2,1,0:T(8,128)(2,1)}), bf16[8,256,768]{2,1,0:T(8,128)(2,1)S(1)}, u32[]{:S(2)}, u32[]{:S(2)}) %all-to-all-start.3) | async-done | bytes 3145760 | tf_op jit(solution)/shard_map/all_to_all | solution.py:608
  404.1 1.7 copy-done
  405.7 12.0 %block_result.1 = bf16[968,768]{1,0:T(8,128)(2,1)} custom-call(bf16[2048,768]{1,0:T(8,128)(2,1)} %bitcast.48, s32[968,2]{1,0:T(8,128)} %get-tuple-element.76.slot_ref, s32[968,2]{1,0:T(8,128)} %copy.54.cols_ref.choice_ref, f32[968,128]{1,0:T(8,128)} %get-tuple-element.77.probs_ref, f32[968,768]{1,0:T(8,128)} %get-tuple-element.78.middle_ref), custom_call_target="tpu_custom_call" | custom-call | tf_op jit(solution)/shard_map/block_result/pallas_call | solution.py:603
  417.7 10.9 %input_grad.1 = (bf16[968,768]{1,0:T(8,128)(2,1)}, f32[2,768]{1,0:T(2,128)}) custom-call(bf16[968,256]{1,0:T(8,128)(2,1)} %get-tuple-element.89.refs_0_, bf16[968,256]{1,0:T(8,128)(2,1)} %get-tuple-element.90.refs_1_, bf16[968,256]{1,0:T(8,128)(2,1)} %get-tuple-element.91.refs_2_, bf16[968,256]{1,0:T(8,128)(2,1)} %get-tuple-element.92.refs_3_, ...), custom_call_target="tpu_custom_call" | custom-call | tf_op jit(solution)/shard_map/input_grad/pallas_call | solution.py:577
  428.6 0.7 pad_maximum_fusion.4
  429.4 51.2 %all-reduce.1 = (f32[7,768]{1,0:T(8,128)S(1)}, f32[768,8]{1,0:T(8,128)S(1)}) all-reduce(f32[7,768]{1,0:T(8,128)S(1)} %pad_maximum_fusion.4, f32[768,8]{1,0:T(8,128)S(1)} %bitcast.68), channel_id=1, replica_groups=mesh['dp'=4,'expert'=8] {'dp','expert'}, use_global_device_ids=true, to_apply=%region_0.1 | all-reduce | flops 11520 | bytes 92160 | tf_op jit(solution)/shard_map/psum | solution.py:694
  480.5 0.7 copy.61
  481.3 0.7 slice_reduce_fusion
  481.9 131.4 %all-reduce.5.cloned.1.call-done = (bf16[3,768,256]{2,1,0:T(8,128)(2,1)}, bf16[3,768,256]{2,1,0:T(8,128)(2,1)}, bf16[3,768,256]{2,1,0:T(8,128)(2,1)}, bf16[768,768]{1,0:T(8,128)(2,1)}) async-done(((bf16[3,768,256]{2,1,0:T(8,128)(2,1)}, bf16[3,768,256]{2,1,0:T(8,128)(2,1)}, bf16[3,768,256]{2,1,0:T(8,128)(2,1)}, bf16[768,768]{1,0:T(8,128)(2,1)}), (bf16[3,768,256]{2,1,0:T(8,128)(2,1)}, ...) | async-done | bytes 4718608 | tf_op jit(solution)/shard_map/psum | solution.py:689
  613.3 3.0 convert_element_type.35
  616.3 0.6 maximum_convert_fusion
  616.9 3.1 slice_bitcast_fusion
  620.1 2.8 convert_element_type.41
  622.9 2.9 convert_element_type.37
  (52 shorter events, 0.3 us)
Async XLA Ops:
  31.0 41.6 %copy-start.4 = (bf16[2048,768]{1,0:T(8,128)(2,1)S(1)}, bf16[2048,768]{1,0:T(8,128)(2,1)}, u32[]{:S(2)}) copy-start(bf16[2048,768]{1,0:T(8,128)(2,1)} %get-tuple-element.71) | copy-start | bytes 9437188
  113.6 41.9 %all-to-all-start = ((bf16[8,256,768]{2,1,0:T(8,128)(2,1)}), bf16[8,256,768]{2,1,0:T(8,128)(2,1)S(1)}, u32[]{:S(2)}, u32[]{:S(2)}) async-start(bf16[8,256,768]{2,1,0:T(8,128)(2,1)} %bitcast.55), calls=%async_computation | async-start | bytes 6291456 | tf_op jit(solution)/shard_map/all_to_all | solution.py:608
  155.5 1.6 copy-start.2
  229.2 3.8 copy-start.17
  229.2 4.8 copy-start.15
  229.2 41.6 %all-to-all-start.4 = ((bf16[8,256,768]{2,1,0:T(8,128)(2,1)}), bf16[8,256,768]{2,1,0:T(8,128)(2,1)S(1)}, u32[]{:S(2)}, u32[]{:S(2)}) async-start(bf16[8,256,768]{2,1,0:T(8,128)(2,1)} %bitcast.54), calls=%async_computation.4 | async-start | bytes 6291456 | tf_op jit(solution)/shard_map/all_to_all | solution.py:608
  232.9 133.3 %reduce-scatter.15.cloned.1.call-start = ((), (), s32[]{:S(2)}) async-start(), calls=%async_computation.13 | async-start | bytes 245760
  233.9 133.9 %reduce-scatter.13.cloned.1.call-start = ((), (), s32[]{:S(2)}) async-start(), calls=%async_computation.12 | async-start | bytes 983040
  235.3 378.0 %all-reduce.5.cloned.1.call-start = ((), (), s32[]{:S(2)}) async-start(), calls=%async_computation.14 | async-start | bytes 9437184 | tf_op jit(solution)/shard_map/psum | solution.py:689
  270.8 1.7 copy-start.1
  313.0 12.3 %copy-start.11 = (bf16[768,256]{1,0:T(8,128)(2,1)S(1)}, bf16[768,256]{1,0:T(8,128)(2,1)}, u32[]{:S(2)}) copy-start(bf16[768,256]{1,0:T(8,128)(2,1)} %get-tuple-element.108) | copy-start | bytes 1179652
  313.0 12.3 %copy-start.12 = (bf16[768,256]{1,0:T(8,128)(2,1)S(1)}, bf16[768,256]{1,0:T(8,128)(2,1)}, u32[]{:S(2)}) copy-start(bf16[768,256]{1,0:T(8,128)(2,1)} %get-tuple-element.109) | copy-start | bytes 1179652
  313.0 12.3 %copy-start.13 = (bf16[768,256]{1,0:T(8,128)(2,1)S(1)}, bf16[768,256]{1,0:T(8,128)(2,1)}, u32[]{:S(2)}) copy-start(bf16[768,256]{1,0:T(8,128)(2,1)} %get-tuple-element.110) | copy-start | bytes 1179652
  325.3 3.0 copy-start.8
  325.3 3.0 copy-start.9
  325.3 3.0 copy-start.10
  329.5 1.9 copy-start.21
  329.5 290.6 %reduce-scatter.11.cloned.1.call-start = ((), (), s32[]{:S(2)}) async-start(), calls=%async_computation.11 | async-start | bytes 5898240 | tf_op jit(solution)/shard_map/reduce_scatter | solution.py:618
  345.9 1.9 copy-start.3
  345.9 277.0 %reduce-scatter.9.cloned.1.call-start = ((), (), s32[]{:S(2)}) async-start(), calls=%async_computation.10 | async-start | bytes 5898240 | tf_op jit(solution)/shard_map/reduce_scatter | solution.py:618
  362.4 41.6 %all-to-all-start.3 = ((bf16[8,256,768]{2,1,0:T(8,128)(2,1)}), bf16[8,256,768]{2,1,0:T(8,128)(2,1)S(1)}, u32[]{:S(2)}, u32[]{:S(2)}) async-start(bf16[8,256,768]{2,1,0:T(8,128)(2,1)} %bitcast.53), calls=%async_computation.3 | async-start | bytes 6291456 | tf_op jit(solution)/shard_map/all_to_all | solution.py:608
  404.1 1.7 copy-start
  417.7 10.9 %copy-start.16 = (f32[3,768]{1,0:T(4,128)S(1)}, f32[3,768]{1,0:T(4,128)}, u32[]{:S(2)}) copy-start(f32[3,768]{1,0:T(4,128)} %get-tuple-element.104) | copy-start | bytes 27652
  417.7 10.9 %copy-start.18 = (f32[2,256]{1,0:T(2,128)S(1)}, f32[2,256]{1,0:T(2,128)}, u32[]{:S(2)}) copy-start(f32[2,256]{1,0:T(2,128)} %get-tuple-element.103) | copy-start | bytes 6148
  417.7 10.9 %copy-start.19 = (f32[2,256]{1,0:T(2,128)S(1)}, f32[2,256]{1,0:T(2,128)}, u32[]{:S(2)}) copy-start(f32[2,256]{1,0:T(2,128)} %get-tuple-element.102) | copy-start | bytes 6148
  417.7 10.9 %copy-start.20 = (f32[2,256]{1,0:T(2,128)S(1)}, f32[2,256]{1,0:T(2,128)}, u32[]{:S(2)}) copy-start(f32[2,256]{1,0:T(2,128)} %get-tuple-element.101) | copy-start | bytes 6148
  417.7 11.6 %copy-start.14 = (f32[768,128]{1,0:T(8,128)S(1)}, f32[768,128]{1,0:T(8,128)}, u32[]{:S(2)}) copy-start(f32[768,128]{1,0:T(8,128)} %get-tuple-element.115) | copy-start | bytes 1179652
  613.3 3.0 copy-start.5
  613.3 3.0 copy-start.6
  613.3 3.0 copy-start.7
Sparse Core Ops, SparseCore 0:
  236.1 20.9 reduce-scatter.14
  259.5 21.5 reduce-scatter.12
  346.1 91.4 reduce-scatter.10
  439.7 90.8 reduce-scatter.8
Sparse Core Ops, SparseCore 1:
  329.6 283.6 all-reduce.4
